TPU v7x, 256 devices: a whole 4x4x8 slice. The times are simulated.
256 devices in a mesh: front: 4 (over x_hi, core), row: 8 (over z), col: 8 (over y, x_lo).
Axes of the slice: x: 4 (x_hi: 2, x_lo: 2; x = x_hi * 2 + x_lo), y: 4, z: 8, core: 2. Of those that a mesh axis runs over, the one named last changes fastest.
Arguments:
- front_block: float32 [4, 8192, 8192], P('front', 'row', 'col'), as said below
- child_map: int32 [4, 60], replicated, may hold values from 8 to 127, as said below
- parent_entries: float32 [16384, 16384], P(('front', 'row'), 'col'), may hold values from -2 to 2
Outputs:
- parent_front: float32 [16384, 16384], P(('front', 'row'), 'col')
Inputs may be any that keep to these rules, and one draw needn't show every extreme that they name: child_map[f, s] is 2 (s + 4) or one more. Each front_block[f] is symmetric and its leading 512 x 512 block is positive definite.
All inputs are finite; a program needn't handle non-finite values.
Results may differ from a plain program's by a relative error of at most 0.0001.
Values sent between devices are 32-bit elements; how exact they have to be, the bound alone decides.
No kernel may reach another device: no remote copies, remote signals or barrier semaphores. Data moves between devices by JAX's collectives and lax.ppermute only.
A program may use at most 128 MiB of HBM per device.

v0:
```python
import jax
import jax.numpy as jnp
from jax import lax
from jax.sharding import PartitionSpec as P

FRONT = 8192
PANEL = 512
TILE = 128


def broadcast(array, axis, root):
    mine = lax.axis_index(axis) == root
    return lax.psum(jnp.where(mine, array, jnp.zeros_like(array)), axis)


def spread(block, row_bits, col_bits):
    row_count = row_bits.shape[0]
    col_count = col_bits.shape[0]
    halves = jnp.arange(2, dtype=jnp.int32)
    row_tiles = block.reshape(row_count, 1, TILE, col_count * TILE)
    doubled = jnp.where(
        row_bits.reshape(row_count, 1, 1, 1) == halves.reshape(1, 2, 1, 1), row_tiles, 0.0
    )
    doubled = doubled.reshape(2 * row_count * TILE, col_count, 1, TILE)
    widened = jnp.where(
        col_bits.reshape(1, col_count, 1, 1) == halves.reshape(1, 1, 2, 1), doubled, 0.0
    )
    return widened.reshape(2 * row_count * TILE, 2 * col_count * TILE)


def lookup(table, index):
    positions = jnp.arange(table.shape[-1], dtype=jnp.int32)
    return jnp.sum(jnp.where(index[..., None] == positions, jnp.expand_dims(table, -2), 0), axis=-1)


def local(front_block, child_map, parent_entries):
    matrix = front_block[0]
    rows_local, cols_local = matrix.shape
    n_front = lax.axis_size("front")
    n_row = lax.axis_size("row")
    my_front = lax.axis_index("front")
    my_row = lax.axis_index("row")
    my_col = lax.axis_index("col")
    panel_cols = broadcast(matrix[:, :PANEL], "col", 0)
    panel_top, pivot_block = (
        broadcast(matrix[:PANEL, :], "row", 0),
        broadcast(panel_cols[:PANEL, :], "row", 0),
    )
    pivot_factor = jnp.linalg.cholesky(pivot_block)
    lower_panel = jax.scipy.linalg.solve_triangular(pivot_factor, panel_cols.T, lower=True).T
    upper_panel = jax.scipy.linalg.solve_triangular(pivot_factor, panel_top, lower=True)
    schur_block = matrix - jnp.dot(
        lower_panel,
        upper_panel,
        precision=lax.Precision.HIGHEST,
        preferred_element_type=jnp.float32,
    )
    tile_total = FRONT // TILE
    pivot_tiles = PANEL // TILE
    sibling_count = child_map.shape[0]
    all_bits = jnp.concatenate(
        [
            -jnp.ones((sibling_count, pivot_tiles), jnp.int32),
            child_map
            - 2 * (jnp.arange(tile_total - pivot_tiles, dtype=jnp.int32) + pivot_tiles)[None, :],
        ],
        axis=1,
    )
    row_tiles = rows_local // TILE
    piece_rows = rows_local // n_front
    piece_tiles = row_tiles // n_front
    col_tiles = cols_local // TILE
    pieces = schur_block.reshape(n_front, piece_rows, cols_local)
    stride = n_row // n_front
    first_row = my_row // n_front
    slot_start = my_row * n_front % n_row
    buffer = lax.dynamic_update_slice_in_dim(
        jnp.zeros((n_row, piece_rows, cols_local), jnp.float32), pieces, slot_start, 0
    )
    arrived = lax.all_to_all(buffer, "row", split_axis=0, concat_axis=0, tiled=True)
    chosen = lax.dynamic_index_in_dim(
        arrived.reshape(n_front, stride, piece_rows, cols_local), first_row, 1, keepdims=False
    )
    piece_index = my_row - first_row * n_front
    within_piece = jnp.arange(piece_tiles, dtype=jnp.int32)
    col_index = my_col * col_tiles + jnp.arange(col_tiles, dtype=jnp.int32)
    my_bits = lax.dynamic_index_in_dim(all_bits, my_front, 0, keepdims=False)
    source_rows = first_row + jnp.arange(n_front, dtype=jnp.int32) * stride
    row_index = source_rows[:, None] * row_tiles + piece_index * piece_tiles + within_piece[None, :]
    row_bits = lookup(my_bits, row_index)
    col_bits = lookup(my_bits, col_index)
    expanded = jax.vmap(spread, in_axes=(0, 0, None))(chosen, row_bits, col_bits)
    summed = lax.psum_scatter(
        expanded.reshape(n_front * 2 * piece_rows, 2 * cols_local),
        "front",
        scatter_dimension=0,
        tiled=True,
    )
    return parent_entries + summed


def solution(mesh):
    in_specs = (P("front", "row", "col"), P(), P(("front", "row"), "col"))
    out_specs = P(("front", "row"), "col")
    return jax.shard_map(local, mesh=mesh, in_specs=in_specs, out_specs=out_specs, check_vma=False)
```

profile of v0, /device:TPU:91, one launch (start us, length us, event | category | flops | bytes accessed | tf_op | source)
XLA Modules:
  0.0 785.1 jit_solution(1421137515406866921)
XLA Ops:
  6.5 5.3 copy.41
  11.9 3.2 slice_select_fusion
  15.1 3.2 select_bitcast_fusion
  18.3 105.3 %all-reduce.6.cloned.1.call-done = f32[1024,512]{0,1:T(8,128)} async-done(((f32[1024,512]{0,1:T(8,128)}), f32[1024,512]{0,1:T(8,128)}) %all-reduce.6.cloned.1.call-update) | async-done | bytes 2097168 | tf_op jit(solution)/shard_map/psum | solution.py:13
  123.7 2.3 slice_select_fusion.1
  126.0 93.3 %all-reduce.8.cloned.1.call-done = (f32[512,512]{0,1:T(8,128)}, f32[512,1024]{1,0:T(8,128)}) async-done(((f32[512,512]{0,1:T(8,128)}, f32[512,1024]{1,0:T(8,128)}), (f32[512,512]{0,1:T(8,128)}, f32[512,1024]{1,0:T(8,128)})) %all-reduce.8.cloned.1.call-update) | async-done | bytes 3145744 | tf_op jit(solution)/shard_map/psum | solution.py:13
  221.3 11.7 %cholesky.103 = f32[128,128]{1,0:T(8,128)S(1)} custom-call(f32[128,128]{1,0:T(8,128)S(1)} %cholesky.263), custom_call_target="Cholesky" | custom-call | tf_op jit(solution)/shard_map/jit(cholesky)/cholesky | solution.py:49
  233.0 9.8 %custom-call.30 = f32[1,128,128]{1,2,0:T(8,128)S(1)} custom-call(f32[1,128,128]{2,1,0:T(8,128)S(1)} %get-tuple-element.71), custom_call_target="InvertDiagBlocksLowerTriangular" | custom-call | tf_op jit(solution)/shard_map/jit(cholesky)/cholesky | solution.py:49
  243.5 11.7 %cholesky.215 = f32[128,128]{1,0:T(8,128)S(1)} custom-call(f32[128,128]{1,0:T(8,128)S(1)} %cholesky.267), custom_call_target="Cholesky" | custom-call | tf_op jit(solution)/shard_map/jit(cholesky)/cholesky | solution.py:49
  255.6 10.1 %custom-call.31 = f32[1,128,128]{1,2,0:T(8,128)S(1)} custom-call(f32[1,128,128]{2,1,0:T(8,128)S(1)} %get-tuple-element.69), custom_call_target="InvertDiagBlocksLowerTriangular" | custom-call | tf_op jit(solution)/shard_map/jit(cholesky)/cholesky | solution.py:49
  266.8 11.7 %cholesky.236 = f32[128,128]{1,0:T(8,128)S(1)} custom-call(f32[128,128]{1,0:T(8,128)S(1)} %cholesky.272), custom_call_target="Cholesky" | custom-call | tf_op jit(solution)/shard_map/jit(cholesky)/cholesky | solution.py:49
  278.7 9.8 %custom-call.32 = f32[1,128,128]{1,2,0:T(8,128)S(1)} custom-call(f32[1,128,128]{2,1,0:T(8,128)S(1)} %get-tuple-element.67), custom_call_target="InvertDiagBlocksLowerTriangular" | custom-call | tf_op jit(solution)/shard_map/jit(cholesky)/cholesky | solution.py:49
  289.3 11.8 %cholesky.253 = f32[128,128]{1,0:T(8,128)S(1)} custom-call(f32[128,128]{1,0:T(8,128)S(1)} %convolution_subtract_fusion.7), custom_call_target="Cholesky" | custom-call | tf_op jit(solution)/shard_map/jit(cholesky)/cholesky | solution.py:49
  306.0 8.3 %while.4 = (s32[]{:T(128)}, f32[512,512]{0,1:T(8,128)S(1)}, s32[4,2]{0,1:T(2,128)S(1)}, f32[4,128,128]{2,1,0:T(8,128)S(1)}, s32[]{:T(128)}) while((s32[]{:T(128)}, f32[512,512]{0,1:T(8,128)S(1)}, s32[4,2]{0,1:T(2,128)S(1)}, f32[4,128,128]{2,1,0:T(8,128)S(1)}, s32[]{:T(128)}) %tuple.36), condition=%wide.while_cond, body=%wide.while_body.sunk | while | flops 2 | bytes 393321 | solution.py:50
  314.2 39.3 %custom-call.34 = f32[4,128,128]{1,2,0:T(8,128)S(1)} custom-call(f32[4,128,128]{2,1,0:T(8,128)S(1)} %get-tuple-element.20), custom_call_target="InvertDiagBlocksLowerTriangular" | custom-call | tf_op jit(solution)/shard_map/jit(_solve_triangular)/triangular_solve | solution.py:50
  355.2 1.7 convolution_subtract_fusion.3
  357.6 1.8 convolution_subtract_fusion.1
  360.0 2.3 fusion.26
  368.1 8.8 %convolution_subtract_fusion = f32[1024,1024]{0,1:T(8,128)} fusion(f32[128,1024]{1,0:T(8,128)S(1)} %fusion.63, f32[128,1024]{1,0:T(8,128)S(1)} %fusion.61, f32[128,1024]{1,0:T(8,128)S(1)} %fusion.59, f32[128,1024]{1,0:T(8,128)S(1)} %fusion.41, f32[128,1024]{1,0:T(8,128)S(1)} %fusion.62, f32[128,1024]{1,0:T(8,128)S(1)} %fusion.60, ...), kind=kOutput, calls=%fused_computation.4 | convolution fusion | flops 6446645248 | bytes 12582912 | tf_op jit(solution)/shard_map/dot_general | solution.py:52
  376.8 5.3 copy.57
  382.2 4.3 broadcast_in_dim.114
  386.5 2.2 constant_dynamic-update-slice_fusion.1
  388.7 5.9 all-to-all-start
  395.3 179.9 %all-to-all-done = f32[8,256,1024]{2,1,0:T(8,128)} async-done(((f32[8,256,1024]{2,1,0:T(8,128)}), f32[8,256,1024]{2,1,0:T(8,128)}, u32[]{:S(2)}, u32[]{:S(2)}) %all-to-all-start) | async-done | bytes 8388640 | tf_op jit(solution)/shard_map/all_to_all | solution.py:80
  575.2 2.8 constant_dynamic-slice_fusion.1
  579.1 2.1 copy.59
  581.2 8.3 %bitcast_select_fusion = f32[4,512,8,128]{3,2,1,0:T(8,128)} fusion(pred[4,512]{1,0:T(4,128)(4,1)S(1)} %bitcast.88, f32[4,512,8,128]{3,2,1,0:T(8,128)S(1)} %bitcast.80), kind=kLoop, calls=%fused_computation.2 | loop fusion | flops 2097152 | bytes 16779264 | tf_op jit(solution)/shard_map/vmap(jit(_where))/select_n | solution.py:21
  589.5 9.1 %broadcast_in_dim.122 = f32[4,512,8,2,128]{4,3,2,1,0:T(2,128)} broadcast(f32[4,512,8,128]{3,2,1,0:T(8,128)} %bitcast_select_fusion), dimensions={0,1,2,4} | broadcast | bytes 25165824 | tf_op jit(solution)/shard_map/vmap(jit(_where))/broadcast_in_dim | solution.py:25
  598.6 21.6 %broadcast_in_dim.123 = f32[2048,2048]{1,0:T(8,128)} reshape(f32[4,512,8,2,128]{4,3,2,1,0:T(2,128)} %broadcast_in_dim.122) | data formatting | bytes 33554432 | tf_op jit(solution)/shard_map/vmap(jit(_where))/broadcast_in_dim | solution.py:25
  620.2 11.8 %broadcast_select_fusion = f32[2048,2048]{1,0:T(8,128)} fusion(f32[2048,2048]{1,0:T(8,128)} %broadcast_in_dim.123, pred[2048]{0:T(1024)(128)(4,1)S(1)} %broadcast_in_dim.107), kind=kLoop, calls=%fused_computation.3 | loop fusion | flops 4194304 | bytes 33556480 | tf_op jit(solution)/shard_map/vmap(jit(_where))/select_n | solution.py:25
  632.0 139.6 %reduce-scatter.2.cloned.1.call-done = f32[512,2048]{1,0:T(8,128)} async-done(((f32[2048,2048]{1,0:T(8,128)}), f32[512,2048]{1,0:T(8,128)}) %reduce-scatter.2.cloned.1.call-update) | async-done | bytes 4194320 | tf_op jit(solution)/shard_map/reduce_scatter | solution.py:93
  771.6 6.6 add.143
  (93 shorter events, 25.8 us)
Async XLA Ops:
  6.5 117.1 %all-reduce.6.cloned.1.call-start = ((), (), s32[]{:S(2)}) async-start(), calls=%async_computation.2 | async-start | bytes 4194304 | tf_op jit(solution)/shard_map/psum | solution.py:13
  15.1 204.3 %all-reduce.8.cloned.1.call-start = ((), (), s32[]{:S(2)}) async-start(), calls=%async_computation.4 | async-start | bytes 6291456 | tf_op jit(solution)/shard_map/psum | solution.py:13
  219.4 1.7 copy-start.3
  360.0 3.0 copy-start.2
  365.6 2.4 copy-start
  382.2 4.3 copy-start.1
  388.7 5.9 copy-start.4
  388.7 186.5 %all-to-all-start = ((f32[8,256,1024]{2,1,0:T(8,128)}), f32[8,256,1024]{2,1,0:T(8,128)}, u32[]{:S(2)}, u32[]{:S(2)}) async-start(f32[8,256,1024]{2,1,0:T(8,128)} %constant_dynamic-update-slice_fusion.1), calls=%async_computation | async-start | bytes 16777216 | tf_op jit(solution)/shard_map/all_to_all | solution.py:80
  394.6 377.0 %reduce-scatter.2.cloned.1.call-start = ((), (), s32[]{:S(2)}) async-start(), calls=%async_computation.3 | async-start | bytes 20971520 | tf_op jit(solution)/shard_map/reduce_scatter | solution.py:93
Sparse Core Ops, SparseCore 0:
  15.2 108.4 all-reduce.5
  126.1 93.2 all-reduce.7
  632.2 139.3 reduce-scatter.1
where the time goes:
time: 798 us; the launch traced here: 785 us
  waiting for transfers between devices  518 us (65%)
  other arithmetic  154 us (19%)
  local copies, waits for them, and re-layouts  64.5 us (8%)
  matrix products  25.4 us (3%)
  between operations  16.4 us (2%)
    psum x2, waiting for transfers between devices, broadcast(): return lax.psum(jnp.where(mine, array, jnp.zeros_like(array)), axis)  199 us
    all_to_all x1, waiting for transfers between devices, local(): lax.all_to_all(buffer, 'row', split_axis=0, concat_axis=0, tiled=True)  180 us
    reduce_scatter x1, waiting for transfers between devices, local(): lax.psum_scatter(expanded.reshape(n_front * 2 * piece_rows, 2 * cols_loca...  140 us
    another operation x14, other arithmetic, local(): pivot_factor = jnp.linalg.cholesky(pivot_block)  78.9 us
    another operation x4, other arithmetic, local(): jax.scipy.linalg.solve_triangular(pivot_factor, panel_cols.T, lower=True)  39.5 us
    broadcast_in_dim x4, local copies, waits for them, and re-layouts, spread(): jnp.where(col_bits.reshape(1, col_count, 1, 1) == halves.reshape(1, 1, 2,...  30.8 us
  transfers between devices with their start and end apart: 4, of which 4 were waited for; matrix products, arithmetic and copies ran while one was open for 0% of the time, Pallas kernels for 0%

commit v1 on v0

v1 whole, which is shorter than its diff:
```python
import functools

import jax
import jax.numpy as jnp
from jax import lax
from jax.experimental import pallas as pl
from jax.experimental.pallas import tpu as pltpu
from jax.sharding import PartitionSpec as P

PANEL = 512
TILE = 128
FRONT_AXES = ("front", "row")
PLANE_AXES = ("row", "col")
PIECES = 4
PIECE = 256
HIGHEST = lax.Precision.HIGHEST
HIGH = lax.Precision.HIGH


def eliminate(block):
    groups = TILE // 8
    tiles = [block[8 * i : 8 * i + 8, :] for i in range(groups)]
    lane = lax.broadcasted_iota(jnp.int32, (8, TILE), 1)
    sublane = lax.broadcasted_iota(jnp.int32, (8, TILE), 0)
    for j in range(TILE):
        t, s = j // 8, j % 8
        row = tiles[t][s : s + 1, :]
        inverse = 1.0 / jnp.broadcast_to(row[:, j : j + 1], (8, TILE))
        here = lane == j
        for i in range(t, groups):
            factor = jnp.broadcast_to(tiles[i][:, j : j + 1], (8, TILE)) * inverse
            new = jnp.where(here, -factor, tiles[i] - factor * row)
            tiles[i] = jnp.where(sublane > s, new, tiles[i]) if i == t else new
    out = []
    for i in range(groups):
        at = sublane + 8 * i
        pivot = jnp.sum(jnp.where(lane == at, tiles[i], 0.0), axis=1, keepdims=True)
        unit = jnp.where(lane < at, tiles[i], jnp.where(lane == at, 1.0, 0.0))
        out.append(unit * lax.rsqrt(pivot))
    return jnp.concatenate(out, axis=0)


def factor_kernel(pivot_ref, out_ref, work):
    rows = lax.broadcasted_iota(jnp.int32, (PANEL, PANEL), 0)
    columns = lax.broadcasted_iota(jnp.int32, (PANEL, PANEL), 1)
    work[:, :PANEL] = pivot_ref[...]
    work[:, PANEL:] = jnp.where(rows == columns, 1.0, 0.0)

    def step(k, carry):
        start = pl.multiple_of(k * TILE, TILE)
        inverse = eliminate(work[pl.ds(start, TILE), pl.ds(start, TILE)])
        solved = jnp.dot(
            inverse,
            work[pl.ds(start, TILE), :],
            precision=HIGHEST,
            preferred_element_type=jnp.float32,
        )
        left = solved[:, :PANEL]
        column = lax.broadcasted_iota(jnp.int32, left.shape, 1)
        left = jnp.where(column >= start + TILE, left, 0.0)
        work[...] -= lax.dot_general(
            left,
            solved,
            (((0,), (0,)), ((), ())),
            precision=HIGHEST,
            preferred_element_type=jnp.float32,
        )
        work[pl.ds(start, TILE), :] = solved
        return carry

    lax.fori_loop(0, PANEL // TILE, step, 0)
    out_ref[...] = work[:, PANEL:]


def inverse_factor(pivot_block):
    return pl.pallas_call(
        factor_kernel,
        out_shape=jax.ShapeDtypeStruct((PANEL, PANEL), jnp.float32),
        in_specs=[pl.BlockSpec(memory_space=pltpu.VMEM)],
        out_specs=pl.BlockSpec(memory_space=pltpu.VMEM),
        scratch_shapes=[pltpu.VMEM((PANEL, 2 * PANEL), jnp.float32)],
        compiler_params=pltpu.CompilerParams(vmem_limit_bytes=24 * 2**20),
        cost_estimate=pl.CostEstimate(
            flops=10_000_000_000, bytes_accessed=2 * 2**20, transcendentals=0
        ),
        name="inverse_factor",
    )(pivot_block)


def extend_add_kernel(place_ref, map_ref, parent_ref, *refs):
    pieces, out_ref = refs[:PIECES], refs[PIECES]
    my_front, my_row, my_col = place_ref[0], place_ref[1], place_ref[2]
    local_row, group = pl.program_id(0), pl.program_id(1)
    col_tiles = pieces[0].shape[1] // TILE
    pivot_tiles = PANEL // TILE

    def bit(front, tile):
        found = map_ref[front, jnp.maximum(tile - pivot_tiles, 0)] - 2 * tile
        return jnp.where(tile >= pivot_tiles, found, -1)

    row_tile = 2 * (8 * my_front + my_row) + local_row
    fronts = [my_front ^ (my_row & 3) ^ k for k in range(PIECES)]
    row_bits = [bit(front, row_tile) for front in fronts]
    for u in range(col_tiles):
        col_tile = 8 * my_col + group * col_tiles + u
        col_bits = [bit(front, col_tile) for front in fronts]
        blocks = [piece[:, u * TILE : (u + 1) * TILE] for piece in pieces]
        for a in range(2):
            for b in range(2):
                rows = slice(a * TILE, (a + 1) * TILE)
                columns = slice((2 * u + b) * TILE, (2 * u + b + 1) * TILE)
                total = parent_ref[rows, columns]
                for k in range(PIECES):
                    hit = jnp.logical_and(row_bits[k] == a, col_bits[k] == b)
                    total += jnp.where(hit, blocks[k], 0.0)
                out_ref[rows, columns] = total


def extend_add(place, child_map, parent, pieces):
    groups = 2
    rows, columns = pieces[0].shape
    wide = columns // groups
    piece_spec = pl.BlockSpec((TILE, wide), lambda i, g, *_: (i, g))
    parent_spec = pl.BlockSpec((2 * TILE, 2 * wide), lambda i, g, *_: (i, g))
    return pl.pallas_call(
        extend_add_kernel,
        out_shape=jax.ShapeDtypeStruct(parent.shape, jnp.float32),
        grid_spec=pltpu.PrefetchScalarGridSpec(
            num_scalar_prefetch=2,
            grid=(rows // TILE, groups),
            in_specs=[parent_spec] + [piece_spec] * PIECES,
            out_specs=parent_spec,
        ),
        cost_estimate=pl.CostEstimate(
            flops=8 * 2**20, bytes_accessed=12 * 2**20, transcendentals=0
        ),
        name="extend_add",
    )(place, child_map, parent, *pieces)


def fan_out(parts, axis, numbers):
    received = [lax.ppermute(parts[k], axis, [numbers(k)]) for k in range(1, 8)]
    return functools.reduce(jnp.add, received)


def local(front_block, child_map, parent_entries):
    matrix = front_block[0]
    my_front = lax.axis_index("front")
    my_row = lax.axis_index("row")
    my_col = lax.axis_index("col")
    quarter = my_row & 3
    chunk = PANEL // 8

    with jax.named_scope("pivot_spread"):
        parts = [matrix[chunk * k : chunk * (k + 1), :PANEL] for k in range(8)]
        part = fan_out(parts, PLANE_AXES, lambda k: (0, k))
        part = jnp.where(my_col == 0, parts[0], part)
        far = fan_out([part] * 8, "row", lambda k: (0, k))
        part = jnp.where(my_row == 0, part, far)
        pivot_block = lax.all_gather(part, "col", tiled=True)

    with jax.named_scope("panel_spread"):
        parts = [matrix[chunk * k : chunk * (k + 1), :] for k in range(8)]
        part = fan_out(parts, "row", lambda k: (0, k))
        part = jnp.where(my_row == 0, parts[0], part)
        panel_top = lax.all_gather(part, "row", tiled=True)

    with jax.named_scope("row_panel"):
        half = my_col & 1
        start = PIECE * quarter
        mine = lax.dynamic_slice_in_dim(panel_top, start + TILE * half, TILE, 1)
        other = lax.dynamic_slice_in_dim(panel_top, start + TILE * (1 - half), TILE, 1)
        pairs = [
            (r * 8 + 2 * y + r // 4, r * 8 + 2 * y + 1 - r // 4) for r in range(8) for y in range(4)
        ]
        other = lax.ppermute(other, PLANE_AXES, pairs)
        mine = jnp.where(half == my_row // 4, mine, other)
        row_panel = lax.all_gather(mine, "col")

    with jax.named_scope("rows_along_z"):
        arrived = []
        for k in range(PIECES):
            piece = (my_row // 2) ^ k ^ my_front
            sent = lax.dynamic_slice_in_dim(matrix, piece * PIECE, PIECE, 0)
            pairs = [
                (f * 8 + r, f * 8 + 4 * (r % 2) + ((r // 2) ^ k ^ f))
                for f in range(4)
                for r in range(8)
            ]
            arrived.append(lax.ppermute(sent, FRONT_AXES, pairs))

    with jax.named_scope("factor"):
        inverse = inverse_factor(pivot_block)
    with jax.named_scope("solve"):
        upper = jnp.dot(inverse, panel_top, precision=HIGH, preferred_element_type=jnp.float32)
        lower = lax.dot_general(
            row_panel,
            inverse,
            (((1,), (1,)), ((), ())),
            precision=HIGH,
            preferred_element_type=jnp.float32,
        ).reshape(PIECES * PIECE, PANEL)

    pieces = []
    for k in range(PIECES):
        with jax.named_scope("schur"):
            target = quarter ^ k ^ my_front
            left = lax.dynamic_slice_in_dim(lower, target * PIECE, PIECE, 0)
            schur = arrived[k] - jnp.dot(
                left, upper, precision=HIGH, preferred_element_type=jnp.float32
            )
        with jax.named_scope("to_parent"):
            pairs = [(f * 8 + r, (f ^ (r & 3) ^ k) * 8 + r) for f in range(4) for r in range(8)]
            pieces.append(lax.ppermute(schur, FRONT_AXES, pairs))

    with jax.named_scope("extend_add"):
        place = jnp.stack([my_front, my_row, my_col]).astype(jnp.int32)
        return extend_add(place, child_map, parent_entries, pieces)


def solution(mesh):
    in_specs = (P("front", "row", "col"), P(), P(("front", "row"), "col"))
    out_specs = P(("front", "row"), "col")
    return jax.shard_map(local, mesh=mesh, in_specs=in_specs, out_specs=out_specs, check_vma=False)
```

time: 798 us -> 290 us (0.36); the launches traced: 785 us -> 287 us
  waiting for transfers between devices: 518 us -> 104 us
  other arithmetic: 154 us -> 5.8 us
  Pallas kernels: 0 us -> 84 us
  local copies, waits for them, and re-layouts: 64.5 us -> 11.4 us
  starting transfers between devices: 5.93 us -> 51.2 us
  matrix products: 25.4 us -> 16.3 us
    psum x2 -> x0, waiting for transfers between devices: 199 us -> none  [broadcast(): return lax.psum(jnp.where(mine, array, jnp.zeros_like(array)), axis)]
    all_to_all x1 -> x0, waiting for transfers between devices: 180 us -> none  [local(): lax.all_to_all(buffer, 'row', split_axis=0, concat_axis=0, tiled=True)]
    reduce_scatter x1 -> x0, waiting for transfers between devices: 140 us -> none  [local(): lax.psum_scatter(expanded.reshape(n_front * 2 * piece_rows, 2 * cols_loca...]
    another operation x18 -> x1, other arithmetic: 118 us -> 0.59 us  [local(): place = jnp.stack([my_front, my_row, my_col]).astype(jnp.int32)]
    pallas_call x0 -> x2, Pallas kernels: none -> 84 us  [the longest x1 77 us: inverse_factor(): pl.pallas_call(factor_kernel, out_shape=jax.ShapeDtypeStruct((PANEL, PANE...]
    ppermute x0 -> x30, waiting for transfers between devices: none -> 83.8 us  [the longest x4 39.2 us: local(): pieces.append(lax.ppermute(schur, FRONT_AXES, pairs))]
    ppermute x0 -> x30, starting transfers between devices: none -> 51.1 us  [the longest x4 18.6 us: local(): arrived.append(lax.ppermute(sent, FRONT_AXES, pairs))]
    broadcast_in_dim x8 -> x0, local copies, waits for them, and re-layouts: 36.3 us -> none  [the longest x4 30.8 us: spread(): jnp.where(col_bits.reshape(1, col_count, 1, 1) == halves.reshape(1, 1, 2,...]
  transfers between devices with their start and end apart: 4 -> 33, of which waited for: 4 -> 7; matrix products, arithmetic and copies ran while one was open for 0% -> 9% of each run, Pallas kernels for 0% -> 27%
where the time goes in v1:
time: 290 us; the launch traced here: 287 us
  waiting for transfers between devices  104 us (36%)
  Pallas kernels  84 us (29%)
  starting transfers between devices  51.2 us (18%)
  matrix products  16.3 us (6%)
  between operations  13.8 us (5%)
  local copies, waits for them, and re-layouts  11.4 us (4%)
  other arithmetic  5.8 us (2%)
    pallas_call x1, Pallas kernels, inverse_factor(): pl.pallas_call(factor_kernel, out_shape=jax.ShapeDtypeStruct((PANEL, PANE...  77 us
    ppermute x4, waiting for transfers between devices, local(): pieces.append(lax.ppermute(schur, FRONT_AXES, pairs))  39.2 us
    ppermute x21, waiting for transfers between devices, fan_out(): received = [lax.ppermute(parts[k], axis, [numbers(k)]) for k in range(1, 8)]  38.9 us
    ppermute x4, starting transfers between devices, local(): arrived.append(lax.ppermute(sent, FRONT_AXES, pairs))  18.6 us
    ppermute x4, starting transfers between devices, local(): pieces.append(lax.ppermute(schur, FRONT_AXES, pairs))  15.9 us
    ppermute x21, starting transfers between devices, fan_out(): received = [lax.ppermute(parts[k], axis, [numbers(k)]) for k in range(1, 8)]  15.3 us
    all_gather x1, waiting for transfers between devices, local(): panel_top = lax.all_gather(part, 'row', tiled=True)  15 us
    dot_general x4, matrix products, local(): jnp.dot(left, upper, precision=HIGH, preferred_element_type=jnp.float32)  9.42 us
  transfers between devices with their start and end apart: 33, of which 7 were waited for; matrix products, arithmetic and copies ran while one was open for 9% of the time, Pallas kernels for 27%

profile of v1, /device:TPU:91, one launch (start us, length us, event | category | flops | bytes accessed | tf_op | source)
XLA Modules:
  0.0 286.6 jit_solution(10314745999416862655)
XLA Ops:
  6.5 1.6 slice_bitcast_fusion.5
  8.8 1.3 collective-permute-start.2
  12.8 9.5 %collective-permute-done.2 = f32[64,1024]{1,0:T(8,128)S(1)} collective-permute-done((f32[64,1024]{1,0:T(8,128)S(1)}, f32[64,1024]{1,0:T(8,128)S(1)}, u32[]{:S(2)}, u32[]{:S(2)}) %collective-permute-start.2) | collective-permute-done | bytes 262176 | tf_op jit(solution)/shard_map/panel_spread/ppermute | solution.py:142
  23.1 1.8 bitcast_select_fusion
  24.9 1.3 fusion.10
  32.8 1.3 collective-permute-start.17
  36.8 29.3 %collective-permute-done.17 = f32[64,512]{1,0:T(8,128)S(1)} collective-permute-done((f32[64,512]{1,0:T(8,128)S(1)}, f32[64,512]{1,0:T(8,128)S(1)}, u32[]{:S(2)}, u32[]{:S(2)}) %collective-permute-start.17) | collective-permute-done | bytes 131104 | tf_op jit(solution)/shard_map/pivot_spread/ppermute | solution.py:142
  67.6 15.0 %all-gather.5.cloned.1.call-done = f32[512,1024]{1,0:T(8,128)} async-done(((f32[64,1024]{1,0:T(8,128)}), f32[512,1024]{1,0:T(8,128)}) %all-gather.5.cloned.1.call-update) | async-done | bytes 2097168 | tf_op jit(solution)/shard_map/panel_spread/all_gather | solution.py:166
  83.6 1.3 collective-permute-start.8
  85.0 5.8 %collective-permute-done.8 = f32[512,128]{1,0:T(8,128)S(1)} collective-permute-done((f32[512,128]{1,0:T(8,128)S(1)}, f32[512,128]{1,0:T(8,128)S(1)}, u32[]{:S(2)}, u32[]{:S(2)}) %collective-permute-start.8) | collective-permute-done | bytes 262176 | tf_op jit(solution)/shard_map/row_panel/ppermute | solution.py:176
  90.7 1.7 dynamic-slice_select_fusion
  92.5 4.4 %dynamic-slice_bitcast_fusion = (f32[256,1024]{1,0:T(8,128)}, f32[256,1024]{1,0:T(8,128)}, f32[256,1024]{1,0:T(8,128)}, f32[256,1024]{1,0:T(8,128)}) fusion(f32[1,1024,1024]{2,1,0:T(8,128)} %param.3, s32[]{:T(128)S(6)} %select_n.89, s32[]{:T(128)S(6)} %select_n.85, s32[]{:T(128)S(6)} %select_n.72, s32[]{:T(128)S(6)} %select_n.87), kind=kLoop, calls=%fused_computation.6 | loop fusion | bytes 8388624 | tf_op jit(solution)/shard_map/rows_along_z/dynamic_slice | solution.py:184
  96.9 1.9 collective-permute-start.28
  98.8 9.4 %collective-permute-start.26 = (f32[256,1024]{1,0:T(8,128)}, f32[256,1024]{1,0:T(8,128)}, u32[]{:S(2)}, u32[]{:S(2)}) collective-permute-start(f32[256,1024]{1,0:T(8,128)} %get-tuple-element.8), channel_id=1, source_target_pairs={{0,16},{8,48},{16,24},{24,56},{32,0},{40,32},{48,8},{56,40},{64,88... | collective-permute-start | bytes 3145736 | tf_op jit(solution)/shard_map/rows_along_z/ppermute | solution.py:190
  108.2 1.9 collective-permute-start.24
  110.1 5.3 %collective-permute-start = (f32[256,1024]{1,0:T(8,128)}, f32[256,1024]{1,0:T(8,128)}, u32[]{:S(2)}, u32[]{:S(2)}) collective-permute-start(f32[256,1024]{1,0:T(8,128)} %get-tuple-element.7), channel_id=1, source_target_pairs={{0,0},{8,32},{16,8},{24,40},{32,16},{40,48},{48,24},{56,56},{64,72... | collective-permute-start | bytes 3145736 | tf_op jit(solution)/shard_map/rows_along_z/ppermute | solution.py:190
  115.5 5.2 %all-gather.7.cloned.1.call-done.pivot_ref = f32[512,512]{1,0:T(8,128)} async-done(((f32[64,512]{1,0:T(8,128)}), f32[512,512]{1,0:T(8,128)}) %all-gather.7.cloned.1.call-update) | async-done | bytes 1048592 | tf_op jit(solution)/shard_map/pivot_spread/all_gather | solution.py:160
  120.7 1.2 copy-done
  121.9 77.0 %inverse_factor.1 = f32[512,512]{1,0:T(8,128)S(1)} custom-call(f32[512,512]{1,0:T(8,128)S(1)} %copy-done), custom_call_target="tpu_custom_call" | custom-call | flops 10000000000 | bytes 2097152 | tf_op jit(solution)/shard_map/factor/inverse_factor/pallas_call | solution.py:76
  199.0 1.8 fusion.11
  200.9 5.0 %fusion = f32[8,128,512]{2,1,0:T(8,128)S(1)} fusion(f32[8,512,128]{2,1,0:T(8,128)} %bitcast.46, f32[512,512]{1,0:T(8,128)S(1)} %inverse_factor.1), kind=kOutput, calls=%fused_computation.4 | convolution fusion | flops 1610612736 | bytes 5242880 | tf_op jit(solution)/shard_map/solve/dot_general | solution.py:196
  205.9 2.4 convolution_subtract_fusion
  208.3 7.0 %collective-permute-start.29 = (f32[256,1024]{1,0:T(8,128)S(1)}, f32[256,1024]{1,0:T(8,128)S(1)}, u32[]{:S(2)}, u32[]{:S(2)}) collective-permute-start(f32[256,1024]{1,0:T(8,128)S(1)} %convolution_subtract_fusion), channel_id=1, source_target_pairs={{0,192},{8,136},{16,80},{24,24},{32,224},{40,168},{48,112},{56,56}... | collective-permute-start | bytes 3145736 | tf_op jit(solution)/shard_map/to_parent/ppermute | solution.py:214
  215.3 2.4 convolution_subtract_fusion.1
  218.4 2.4 convolution_subtract_fusion.2
  220.8 3.8 %collective-permute-start.25 = (f32[256,1024]{1,0:T(8,128)S(1)}, f32[256,1024]{1,0:T(8,128)S(1)}, u32[]{:S(2)}, u32[]{:S(2)}) collective-permute-start(f32[256,1024]{1,0:T(8,128)S(1)} %convolution_subtract_fusion.2), channel_id=1, source_target_pairs={{0,64},{8,8},{16,208},{24,152},{32,96},{40,40},{48,240},{56,184},{... | collective-permute-start | bytes 3145736 | tf_op jit(solution)/shard_map/to_parent/ppermute | solution.py:214
  224.6 2.4 convolution_subtract_fusion.3
  227.0 4.4 %collective-permute-start.23 = (f32[256,1024]{1,0:T(8,128)S(1)}, f32[256,1024]{1,0:T(8,128)S(1)}, u32[]{:S(2)}, u32[]{:S(2)}) collective-permute-start(f32[256,1024]{1,0:T(8,128)S(1)} %convolution_subtract_fusion.3), channel_id=1, source_target_pairs={{0,0},{8,72},{16,144},{24,216},{32,32},{40,104},{48,176},{56,248},... | collective-permute-start | bytes 3145736 | tf_op jit(solution)/shard_map/to_parent/ppermute | solution.py:214
  232.0 17.2 %collective-permute-done.25.refs_1_ = f32[256,1024]{1,0:T(8,128)S(1)} collective-permute-done((f32[256,1024]{1,0:T(8,128)S(1)}, f32[256,1024]{1,0:T(8,128)S(1)}, u32[]{:S(2)}, u32[]{:S(2)}) %collective-permute-start.25) | collective-permute-done | bytes 1048608 | tf_op jit(solution)/shard_map/to_parent/ppermute | solution.py:214
  250.2 22.0 %collective-permute-done.23.refs_0_ = f32[256,1024]{1,0:T(8,128)S(1)} collective-permute-done((f32[256,1024]{1,0:T(8,128)S(1)}, f32[256,1024]{1,0:T(8,128)S(1)}, u32[]{:S(2)}, u32[]{:S(2)}) %collective-permute-start.23) | collective-permute-done | bytes 1048608 | tf_op jit(solution)/shard_map/to_parent/ppermute | solution.py:214
  272.1 1.0 copy-done.5
  273.1 6.9 %extend_add.1 = f32[512,2048]{1,0:T(8,128)} custom-call(s32[3]{0:T(128)} %pad_add_fusion.place_ref, s32[4,60]{1,0:T(4,128)} %map_ref.1, f32[512,2048]{1,0:T(8,128)} %parent_ref.1, f32[256,1024]{1,0:T(8,128)} %copy-done.5, f32[256,1024]{1,0:T(8,128)} %copy-done.4, f32[256,1024]{1,0:T(8,128)} %copy-done.3, f32[256,1024]{1,0:T(8,128)} %copy-done.2), custom_call_target="tpu_custom_call" | custom-call | flops 8388608 | bytes 12582912 | tf_op jit(solution)/shard_map/extend_add/extend_add/pallas_call | solution.py:125
  (66 shorter events, 18.0 us)
Async XLA Ops:
  6.5 76.1 %all-gather.5.cloned.1.call-start = ((), (), s32[]{:S(2)}) async-start(), calls=%async_computation | async-start | bytes 2359296 | tf_op jit(solution)/shard_map/panel_spread/all_gather | solution.py:166
  8.1 4.0 %collective-permute-start.1 = (f32[64,1024]{1,0:T(8,128)S(1)}, f32[64,1024]{1,0:T(8,128)S(1)}, u32[]{:S(2)}, u32[]{:S(2)}) collective-permute-start(f32[64,1024]{1,0:T(8,128)S(1)} %get-tuple-element.15), channel_id=1, source_target_pairs={{0,8},{1,9},{2,10},{3,11},{4,12},{5,13},{6,14},{7,15},{64,72},{65,... | collective-permute-start | bytes 786440 | tf_op jit(solution)/shard_map/panel_spread/ppermute | solution.py:142
  8.8 13.5 %collective-permute-start.2 = (f32[64,1024]{1,0:T(8,128)S(1)}, f32[64,1024]{1,0:T(8,128)S(1)}, u32[]{:S(2)}, u32[]{:S(2)}) collective-permute-start(f32[64,1024]{1,0:T(8,128)S(1)} %get-tuple-element.9), channel_id=1, source_target_pairs={{0,16},{1,17},{2,18},{3,19},{4,20},{5,21},{6,22},{7,23},{64,80},{6... | collective-permute-start | bytes 786440 | tf_op jit(solution)/shard_map/panel_spread/ppermute | solution.py:142
  10.1 12.9 %collective-permute-start.3 = (f32[64,1024]{1,0:T(8,128)S(1)}, f32[64,1024]{1,0:T(8,128)S(1)}, u32[]{:S(2)}, u32[]{:S(2)}) collective-permute-start(f32[64,1024]{1,0:T(8,128)S(1)} %get-tuple-element.14), channel_id=1, source_target_pairs={{0,24},{1,25},{2,26},{3,27},{4,28},{5,29},{6,30},{7,31},{64,88},{6... | collective-permute-start | bytes 786440 | tf_op jit(solution)/shard_map/panel_spread/ppermute | solution.py:142
  10.8 12.3 %collective-permute-start.4 = (f32[64,1024]{1,0:T(8,128)S(1)}, f32[64,1024]{1,0:T(8,128)S(1)}, u32[]{:S(2)}, u32[]{:S(2)}) collective-permute-start(f32[64,1024]{1,0:T(8,128)S(1)} %get-tuple-element.13), channel_id=1, source_target_pairs={{0,32},{1,33},{2,34},{3,35},{4,36},{5,37},{6,38},{7,39},{64,96},{6... | collective-permute-start | bytes 786440 | tf_op jit(solution)/shard_map/panel_spread/ppermute | solution.py:142
  11.5 11.6 %collective-permute-start.5 = (f32[64,1024]{1,0:T(8,128)S(1)}, f32[64,1024]{1,0:T(8,128)S(1)}, u32[]{:S(2)}, u32[]{:S(2)}) collective-permute-start(f32[64,1024]{1,0:T(8,128)S(1)} %get-tuple-element.12), channel_id=1, source_target_pairs={{0,40},{1,41},{2,42},{3,43},{4,44},{5,45},{6,46},{7,47},{64,104},{... | collective-permute-start | bytes 786440 | tf_op jit(solution)/shard_map/panel_spread/ppermute | solution.py:142
  12.2 10.9 %collective-permute-start.6 = (f32[64,1024]{1,0:T(8,128)S(1)}, f32[64,1024]{1,0:T(8,128)S(1)}, u32[]{:S(2)}, u32[]{:S(2)}) collective-permute-start(f32[64,1024]{1,0:T(8,128)S(1)} %get-tuple-element.11), channel_id=1, source_target_pairs={{0,48},{1,49},{2,50},{3,51},{4,52},{5,53},{6,54},{7,55},{64,112},{... | collective-permute-start | bytes 786440 | tf_op jit(solution)/shard_map/panel_spread/ppermute | solution.py:142
  22.3 0.7 collective-permute-start.7
  24.9 95.8 %all-gather.7.cloned.1.call-start = ((), (), s32[]{:S(2)}) async-start(), calls=%async_computation.1 | async-start | bytes 1179648 | tf_op jit(solution)/shard_map/pivot_spread/all_gather | solution.py:160
  26.3 3.4 %collective-permute-start.10 = (f32[64,512]{1,0:T(8,128)S(1)}, f32[64,512]{1,0:T(8,128)S(1)}, u32[]{:S(2)}, u32[]{:S(2)}) collective-permute-start(f32[64,512]{1,0:T(8,128)S(1)} %get-tuple-element.16), channel_id=1, source_target_pairs={{0,2},{64,66},{128,130},{192,194}} | collective-permute-start | bytes 393224 | tf_op jit(solution)/shard_map/pivot_spread/ppermute | solution.py:142
  26.9 3.4 %collective-permute-start.11 = (f32[64,512]{1,0:T(8,128)S(1)}, f32[64,512]{1,0:T(8,128)S(1)}, u32[]{:S(2)}, u32[]{:S(2)}) collective-permute-start(f32[64,512]{1,0:T(8,128)S(1)} %get-tuple-element.21), channel_id=1, source_target_pairs={{0,3},{64,67},{128,131},{192,195}} | collective-permute-start | bytes 393224 | tf_op jit(solution)/shard_map/pivot_spread/ppermute | solution.py:142
  27.6 3.4 %collective-permute-start.12 = (f32[64,512]{1,0:T(8,128)S(1)}, f32[64,512]{1,0:T(8,128)S(1)}, u32[]{:S(2)}, u32[]{:S(2)}) collective-permute-start(f32[64,512]{1,0:T(8,128)S(1)} %get-tuple-element.20), channel_id=1, source_target_pairs={{0,4},{64,68},{128,132},{192,196}} | collective-permute-start | bytes 393224 | tf_op jit(solution)/shard_map/pivot_spread/ppermute | solution.py:142
  28.3 2.7 collective-permute-start.13
  29.0 2.1 collective-permute-start.14
  29.7 1.4 collective-permute-start.15
  30.4 0.7 collective-permute-start.9
  32.1 4.0 %collective-permute-start.16 = (f32[64,512]{1,0:T(8,128)S(1)}, f32[64,512]{1,0:T(8,128)S(1)}, u32[]{:S(2)}, u32[]{:S(2)}) collective-permute-start(f32[64,512]{1,0:T(8,128)S(1)} %slice_select_fusion), channel_id=1, source_target_pairs={{0,8},{1,9},{2,10},{3,11},{4,12},{5,13},{6,14},{7,15},{64,72},{65,... | collective-permute-start | bytes 393224 | tf_op jit(solution)/shard_map/pivot_spread/ppermute | solution.py:142
  32.8 33.3 %collective-permute-start.17 = (f32[64,512]{1,0:T(8,128)S(1)}, f32[64,512]{1,0:T(8,128)S(1)}, u32[]{:S(2)}, u32[]{:S(2)}) collective-permute-start(f32[64,512]{1,0:T(8,128)S(1)} %slice_select_fusion), channel_id=1, source_target_pairs={{0,16},{1,17},{2,18},{3,19},{4,20},{5,21},{6,22},{7,23},{64,80},{6... | collective-permute-start | bytes 393224 | tf_op jit(solution)/shard_map/pivot_spread/ppermute | solution.py:142
  34.1 32.7 %collective-permute-start.18 = (f32[64,512]{1,0:T(8,128)S(1)}, f32[64,512]{1,0:T(8,128)S(1)}, u32[]{:S(2)}, u32[]{:S(2)}) collective-permute-start(f32[64,512]{1,0:T(8,128)S(1)} %slice_select_fusion), channel_id=1, source_target_pairs={{0,24},{1,25},{2,26},{3,27},{4,28},{5,29},{6,30},{7,31},{64,88},{6... | collective-permute-start | bytes 393224 | tf_op jit(solution)/shard_map/pivot_spread/ppermute | solution.py:142
  34.7 32.0 %collective-permute-start.19 = (f32[64,512]{1,0:T(8,128)S(1)}, f32[64,512]{1,0:T(8,128)S(1)}, u32[]{:S(2)}, u32[]{:S(2)}) collective-permute-start(f32[64,512]{1,0:T(8,128)S(1)} %slice_select_fusion), channel_id=1, source_target_pairs={{0,32},{1,33},{2,34},{3,35},{4,36},{5,37},{6,38},{7,39},{64,96},{6... | collective-permute-start | bytes 393224 | tf_op jit(solution)/shard_map/pivot_spread/ppermute | solution.py:142
  35.4 31.4 %collective-permute-start.20 = (f32[64,512]{1,0:T(8,128)S(1)}, f32[64,512]{1,0:T(8,128)S(1)}, u32[]{:S(2)}, u32[]{:S(2)}) collective-permute-start(f32[64,512]{1,0:T(8,128)S(1)} %slice_select_fusion), channel_id=1, source_target_pairs={{0,40},{1,41},{2,42},{3,43},{4,44},{5,45},{6,46},{7,47},{64,104},{... | collective-permute-start | bytes 393224 | tf_op jit(solution)/shard_map/pivot_spread/ppermute | solution.py:142
  36.1 30.7 %collective-permute-start.21 = (f32[64,512]{1,0:T(8,128)S(1)}, f32[64,512]{1,0:T(8,128)S(1)}, u32[]{:S(2)}, u32[]{:S(2)}) collective-permute-start(f32[64,512]{1,0:T(8,128)S(1)} %slice_select_fusion), channel_id=1, source_target_pairs={{0,48},{1,49},{2,50},{3,51},{4,52},{5,53},{6,54},{7,55},{64,112},{... | collective-permute-start | bytes 393224 | tf_op jit(solution)/shard_map/pivot_spread/ppermute | solution.py:142
  67.6 133.3 %all-gather.9.cloned.1.call-start = ((), (), s32[]{:S(2)}) async-start(), calls=%async_computation.2 | async-start | bytes 2359296 | tf_op jit(solution)/shard_map/row_panel/all_gather | solution.py:178
  83.6 7.1 %collective-permute-start.8 = (f32[512,128]{1,0:T(8,128)S(1)}, f32[512,128]{1,0:T(8,128)S(1)}, u32[]{:S(2)}, u32[]{:S(2)}) collective-permute-start(f32[512,128]{1,0:T(8,128)S(1)} %constant_dynamic-slice_fusion), channel_id=1, source_target_pairs={{0,1},{2,3},{4,5},{6,7},{8,9},{10,11},{12,13},{14,15},{16,17},{18,... | collective-permute-start | bytes 786440 | tf_op jit(solution)/shard_map/row_panel/ppermute | solution.py:176
  96.9 109.0 %collective-permute-start.28 = (f32[256,1024]{1,0:T(8,128)}, f32[256,1024]{1,0:T(8,128)}, u32[]{:S(2)}, u32[]{:S(2)}) collective-permute-start(f32[256,1024]{1,0:T(8,128)} %get-tuple-element.5), channel_id=1, source_target_pairs={{0,24},{8,56},{16,16},{24,48},{32,8},{40,40},{48,0},{56,32},{64,80... | collective-permute-start | bytes 3145736 | tf_op jit(solution)/shard_map/rows_along_z/ppermute | solution.py:190
  98.8 116.5 %collective-permute-start.26 = (f32[256,1024]{1,0:T(8,128)}, f32[256,1024]{1,0:T(8,128)}, u32[]{:S(2)}, u32[]{:S(2)}) collective-permute-start(f32[256,1024]{1,0:T(8,128)} %get-tuple-element.8), channel_id=1, source_target_pairs={{0,16},{8,48},{16,24},{24,56},{32,0},{40,32},{48,8},{56,40},{64,88... | collective-permute-start | bytes 3145736 | tf_op jit(solution)/shard_map/rows_along_z/ppermute | solution.py:190
  108.2 110.2 %collective-permute-start.24 = (f32[256,1024]{1,0:T(8,128)}, f32[256,1024]{1,0:T(8,128)}, u32[]{:S(2)}, u32[]{:S(2)}) collective-permute-start(f32[256,1024]{1,0:T(8,128)} %get-tuple-element.6), channel_id=1, source_target_pairs={{0,8},{8,40},{16,0},{24,32},{32,24},{40,56},{48,16},{56,48},{64,64... | collective-permute-start | bytes 3145736 | tf_op jit(solution)/shard_map/rows_along_z/ppermute | solution.py:190
  110.1 114.5 %collective-permute-start = (f32[256,1024]{1,0:T(8,128)}, f32[256,1024]{1,0:T(8,128)}, u32[]{:S(2)}, u32[]{:S(2)}) collective-permute-start(f32[256,1024]{1,0:T(8,128)} %get-tuple-element.7), channel_id=1, source_target_pairs={{0,0},{8,32},{16,8},{24,40},{32,16},{40,48},{48,24},{56,56},{64,72... | collective-permute-start | bytes 3145736 | tf_op jit(solution)/shard_map/rows_along_z/ppermute | solution.py:190
  208.3 23.7 %collective-permute-start.29 = (f32[256,1024]{1,0:T(8,128)S(1)}, f32[256,1024]{1,0:T(8,128)S(1)}, u32[]{:S(2)}, u32[]{:S(2)}) collective-permute-start(f32[256,1024]{1,0:T(8,128)S(1)} %convolution_subtract_fusion), channel_id=1, source_target_pairs={{0,192},{8,136},{16,80},{24,24},{32,224},{40,168},{48,112},{56,56}... | collective-permute-start | bytes 3145736 | tf_op jit(solution)/shard_map/to_parent/ppermute | solution.py:214
  217.7 14.3 %collective-permute-start.27 = (f32[256,1024]{1,0:T(8,128)S(1)}, f32[256,1024]{1,0:T(8,128)S(1)}, u32[]{:S(2)}, u32[]{:S(2)}) collective-permute-start(f32[256,1024]{1,0:T(8,128)S(1)} %convolution_subtract_fusion.1), channel_id=1, source_target_pairs={{0,128},{8,200},{16,16},{24,88},{32,160},{40,232},{48,48},{56,120}... | collective-permute-start | bytes 3145736 | tf_op jit(solution)/shard_map/to_parent/ppermute | solution.py:214
  220.8 28.4 %collective-permute-start.25 = (f32[256,1024]{1,0:T(8,128)S(1)}, f32[256,1024]{1,0:T(8,128)S(1)}, u32[]{:S(2)}, u32[]{:S(2)}) collective-permute-start(f32[256,1024]{1,0:T(8,128)S(1)} %convolution_subtract_fusion.2), channel_id=1, source_target_pairs={{0,64},{8,8},{16,208},{24,152},{32,96},{40,40},{48,240},{56,184},{... | collective-permute-start | bytes 3145736 | tf_op jit(solution)/shard_map/to_parent/ppermute | solution.py:214
  227.0 45.1 %collective-permute-start.23 = (f32[256,1024]{1,0:T(8,128)S(1)}, f32[256,1024]{1,0:T(8,128)S(1)}, u32[]{:S(2)}, u32[]{:S(2)}) collective-permute-start(f32[256,1024]{1,0:T(8,128)S(1)} %convolution_subtract_fusion.3), channel_id=1, source_target_pairs={{0,0},{8,72},{16,144},{24,216},{32,32},{40,104},{48,176},{56,248},... | collective-permute-start | bytes 3145736 | tf_op jit(solution)/shard_map/to_parent/ppermute | solution.py:214
  (7 other events, 138.4 us)
Sparse Core Ops, SparseCore 0:
  25.0 57.5 all-gather.4
  84.4 36.1 all-gather.6
  122.5 57.8 all-gather.8

commit v2 on v1

v2 whole, which is shorter than its diff:
```python
import functools

import jax
import jax.numpy as jnp
from jax import lax
from jax.experimental import pallas as pl
from jax.experimental.pallas import tpu as pltpu
from jax.sharding import PartitionSpec as P

PANEL = 512
TILE = 128
FRONT_AXES = ("front", "row")
PLANE_AXES = ("row", "col")
PIECES = 4
PIECE = 256
HIGHEST = lax.Precision.HIGHEST
HIGH = lax.Precision.HIGH


def eliminate(block):
    groups = TILE // 8
    tiles = [block[8 * i : 8 * i + 8, :] for i in range(groups)]
    sublane = lax.broadcasted_iota(jnp.int32, (8, TILE), 0)
    lanes = lax.broadcasted_iota(jnp.int32, (8, TILE), 1)
    lane = lax.broadcasted_iota(jnp.int32, (1, TILE), 1)
    out = []
    for t in range(groups):
        j = 8 * t
        columns = [
            [jnp.broadcast_to(tiles[i][:, j + k : j + k + 1], (8, TILE)) for k in range(8)]
            for i in range(t, groups)
        ]
        pivots = [[columns[0][k][m : m + 1, :] for k in range(8)] for m in range(8)]
        rows, inverses = [], []
        final = None
        for k in range(8):
            factors = [pivots[m][k] * inverses[m] for m in range(k)]
            for c in range(k, 8):
                for m in range(k):
                    pivots[k][c] -= factors[m] * pivots[m][c]
            inverses.append(1.0 / pivots[k][k])
            unit = jnp.where(lane == j + k, 1.0, 0.0)
            row = jnp.where((lane >= j) & (lane < j + 8), unit, tiles[t][k : k + 1, :])
            for m in range(k):
                row -= factors[m] * rows[m]
            rows.append(row)
            scaled = jnp.where(lane <= j + k, row, 0.0) * lax.rsqrt(pivots[k][k])
            scaled = jnp.broadcast_to(scaled, (8, TILE))
            final = scaled if k == 0 else jnp.where(sublane == k, scaled, final)
        out.append(final)
        for i in range(t + 1, groups):
            factors = []
            new = jnp.where((lanes >= j) & (lanes < j + 8), 0.0, tiles[i])
            for k in range(8):
                value = columns[i - t][k]
                for m in range(k):
                    value -= factors[m] * pivots[m][k]
                factors.append(value * inverses[k])
                new -= factors[k] * rows[k]
            tiles[i] = new
    return jnp.concatenate(out, axis=0)


def exact_dot(left, right, contract):
    return lax.dot_general(
        left,
        right,
        (contract, ((), ())),
        precision=HIGHEST,
        preferred_element_type=jnp.float32,
    )


def factor_kernel(place_ref, *refs):
    parts, out_ref, work = refs[:8], refs[8], refs[9]
    my_col = place_ref[2]
    chunk = PANEL // 8
    for j in range(8):
        start = pl.multiple_of(chunk * (my_col ^ j), chunk)
        work[pl.ds(start, chunk), :] = parts[j][...]
    for k in range(PANEL // TILE):
        low, high = k * TILE, (k + 1) * TILE
        inverse = eliminate(work[low:high, low:high])
        work[low:high, low:high] = inverse
        if k > 0:
            work[low:high, :low] = exact_dot(inverse, work[low:high, :low], ((1,), (0,)))
        if high < PANEL:
            right = exact_dot(inverse, work[low:high, high:], ((1,), (0,)))
            work[low:high, high:] = right
            work[high:, low:high] = jnp.zeros((PANEL - high, TILE), jnp.float32)
            work[high:, :] -= exact_dot(right, work[low:high, :], ((0,), (0,)))
            work[low:high, high:] = jnp.zeros_like(right)
    out_ref[...] = work[...]


def inverse_factor(place, parts):
    return pl.pallas_call(
        factor_kernel,
        out_shape=jax.ShapeDtypeStruct((PANEL, PANEL), jnp.float32),
        in_specs=[pl.BlockSpec(memory_space=pltpu.SMEM)]
        + [pl.BlockSpec(memory_space=pltpu.VMEM)] * 8,
        out_specs=pl.BlockSpec(memory_space=pltpu.VMEM),
        scratch_shapes=[pltpu.VMEM((PANEL, PANEL), jnp.float32)],
        compiler_params=pltpu.CompilerParams(vmem_limit_bytes=24 * 2**20),
        cost_estimate=pl.CostEstimate(
            flops=10_000_000_000, bytes_accessed=2 * 2**20, transcendentals=0
        ),
        name="inverse_factor",
    )(place, *parts)


def split(value):
    high = value.astype(jnp.bfloat16)
    return high, (value - high.astype(jnp.float32)).astype(jnp.bfloat16)


def split_dot(left, right, contract):
    def dot(a, b):
        return lax.dot_general(a, b, (contract, ((), ())), preferred_element_type=jnp.float32)

    return dot(left[0], right[0]) + (dot(left[0], right[1]) + dot(left[1], right[0]))


def solve_kernel(inverse_ref, top_ref, rows_ref, lower_ref, upper_ref):
    inverse = split(inverse_ref[...])
    for j in range(8):
        lower_ref[TILE * j : TILE * (j + 1), :] = split_dot(
            split(rows_ref[j]), inverse, ((0,), (1,))
        )
    wide = 256
    for j in range(0, top_ref.shape[1], wide):
        upper_ref[:, j : j + wide] = split_dot(
            inverse, split(top_ref[:, j : j + wide]), ((1,), (0,))
        )


def solve(inverse, panel_top, row_panel):
    vmem = pl.BlockSpec(memory_space=pltpu.VMEM)
    return pl.pallas_call(
        solve_kernel,
        out_shape=(
            jax.ShapeDtypeStruct((PIECES * PIECE, PANEL), jnp.float32),
            jax.ShapeDtypeStruct(panel_top.shape, jnp.float32),
        ),
        in_specs=[vmem] * 3,
        out_specs=(vmem, vmem),
        compiler_params=pltpu.CompilerParams(vmem_limit_bytes=40 * 2**20),
        cost_estimate=pl.CostEstimate(
            flops=6_000_000_000, bytes_accessed=9 * 2**20, transcendentals=0
        ),
        name="solve",
    )(inverse, panel_top, row_panel)


def extend_add_kernel(place_ref, map_ref, parent_ref, *refs):
    pieces, out_ref = refs[:PIECES], refs[PIECES]
    my_front, my_row, my_col = place_ref[0], place_ref[1], place_ref[2]
    local_row, group = pl.program_id(0), pl.program_id(1)
    col_tiles = pieces[0].shape[1] // TILE
    pivot_tiles = PANEL // TILE

    def bit(front, tile):
        found = map_ref[front, jnp.maximum(tile - pivot_tiles, 0)] - 2 * tile
        return jnp.where(tile >= pivot_tiles, found, -1)

    row_tile = 2 * (8 * my_front + my_row) + local_row
    fronts = [my_front ^ (my_row & 3) ^ k for k in range(PIECES)]
    row_bits = [bit(front, row_tile) for front in fronts]
    for u in range(col_tiles):
        col_tile = 8 * my_col + group * col_tiles + u
        col_bits = [bit(front, col_tile) for front in fronts]
        blocks = [piece[:, u * TILE : (u + 1) * TILE] for piece in pieces]
        for a in range(2):
            for b in range(2):
                rows = slice(a * TILE, (a + 1) * TILE)
                columns = slice((2 * u + b) * TILE, (2 * u + b + 1) * TILE)
                total = parent_ref[rows, columns]
                for k in range(PIECES):
                    hit = jnp.logical_and(row_bits[k] == a, col_bits[k] == b)
                    total += jnp.where(hit, blocks[k], 0.0)
                out_ref[rows, columns] = total


def extend_add(place, child_map, parent, pieces):
    groups = 2
    rows, columns = pieces[0].shape
    wide = columns // groups
    piece_spec = pl.BlockSpec((TILE, wide), lambda i, g, *_: (i, g))
    parent_spec = pl.BlockSpec((2 * TILE, 2 * wide), lambda i, g, *_: (i, g))
    return pl.pallas_call(
        extend_add_kernel,
        out_shape=jax.ShapeDtypeStruct(parent.shape, jnp.float32),
        grid_spec=pltpu.PrefetchScalarGridSpec(
            num_scalar_prefetch=2,
            grid=(rows // TILE, groups),
            in_specs=[parent_spec] + [piece_spec] * PIECES,
            out_specs=parent_spec,
        ),
        cost_estimate=pl.CostEstimate(
            flops=8 * 2**20, bytes_accessed=12 * 2**20, transcendentals=0
        ),
        name="extend_add",
    )(place, child_map, parent, *pieces)


def fan_out(parts, axis, numbers):
    received = [lax.ppermute(parts[k], axis, [numbers(k)]) for k in range(1, 8)]
    return functools.reduce(jnp.add, received)


def local(front_block, child_map, parent_entries):
    matrix = front_block[0]
    my_front = lax.axis_index("front")
    my_row = lax.axis_index("row")
    my_col = lax.axis_index("col")
    quarter = my_row & 3
    chunk = PANEL // 8

    place = jnp.stack([my_front, my_row, my_col]).astype(jnp.int32)

    with jax.named_scope("pivot_to_columns"):
        parts = [matrix[chunk * k : chunk * (k + 1), :PANEL] for k in range(8)]
        part = fan_out(parts, PLANE_AXES, lambda k: (0, k))
        part = jnp.where(my_col == 0, parts[0], part)

    with jax.named_scope("panel_scatter"):
        parts = [matrix[chunk * k : chunk * (k + 1), :] for k in range(8)]
        panel_part = fan_out(parts, "row", lambda k: (0, k))
        panel_part = jnp.where(my_row == 0, parts[0], panel_part)
        part, panel_part = lax.optimization_barrier((part, panel_part))

    with jax.named_scope("pivot_along_z"):
        for distance in (4, 2, 1):
            pairs = [(r, r + distance) for r in range(0, 8, 2 * distance)]
            far = lax.ppermute(part, "row", pairs)
            part = jnp.where((my_row & (2 * distance - 1)) == distance, far, part)

    with jax.named_scope("pivot_in_plane"):
        parts = [part] + [
            lax.ppermute(part, "col", [(c, c ^ j) for c in range(8)]) for j in range(1, 8)
        ]

    with jax.named_scope("panel_gather"):
        panel_top = lax.all_gather(panel_part, "row", tiled=True)

    with jax.named_scope("rows_along_z"):
        panel_top, matrix = lax.optimization_barrier((panel_top, matrix))
        arrived = []
        for k in range(PIECES):
            piece = (my_row // 2) ^ k ^ my_front
            sent = lax.dynamic_slice_in_dim(matrix, piece * PIECE, PIECE, 0)
            pairs = [
                (f * 8 + r, f * 8 + 4 * (r % 2) + ((r // 2) ^ k ^ f))
                for f in range(4)
                for r in range(8)
            ]
            arrived.append(lax.ppermute(sent, FRONT_AXES, pairs))

    with jax.named_scope("row_panel"):
        panel_top, *parts = lax.optimization_barrier((panel_top, *parts))
        half = my_col & 1
        start = PIECE * quarter
        mine = lax.dynamic_slice_in_dim(panel_top, start + TILE * half, TILE, 1)
        other = lax.dynamic_slice_in_dim(panel_top, start + TILE * (1 - half), TILE, 1)
        pairs = [
            (r * 8 + 2 * y + r // 4, r * 8 + 2 * y + 1 - r // 4) for r in range(8) for y in range(4)
        ]
        other = lax.ppermute(other, PLANE_AXES, pairs)
        mine = jnp.where(half == my_row // 4, mine, other)
        row_panel = lax.all_gather(mine, "col")

    with jax.named_scope("factor"):
        inverse = inverse_factor(place, parts)

    with jax.named_scope("solve"):
        lower, upper = solve(inverse, panel_top, row_panel)

    pieces = []
    for k in range(PIECES):
        with jax.named_scope("schur"):
            target = quarter ^ k ^ my_front
            left = lax.dynamic_slice_in_dim(lower, target * PIECE, PIECE, 0)
            schur = arrived[k] - jnp.dot(
                left, upper, precision=HIGH, preferred_element_type=jnp.float32
            )
        with jax.named_scope("to_parent"):
            pairs = [(f * 8 + r, (f ^ (r & 3) ^ k) * 8 + r) for f in range(4) for r in range(8)]
            pieces.append(lax.ppermute(schur, FRONT_AXES, pairs))

    with jax.named_scope("extend_add"):
        return extend_add(place, child_map, parent_entries, pieces)


def solution(mesh):
    in_specs = (P("front", "row", "col"), P(), P(("front", "row"), "col"))
    out_specs = P(("front", "row"), "col")
    return jax.shard_map(local, mesh=mesh, in_specs=in_specs, out_specs=out_specs, check_vma=False)
```

time: 290 us -> 282 us (0.972)
  Pallas kernels: 84 us -> 31.4 us
  starting transfers between devices: 51.2 us -> 78.9 us
  waiting for transfers between devices: 104 us -> 129 us
  matrix products: 16.3 us -> 9.25 us
    pallas_call x1, Pallas kernels: 77 us -> 18.6 us  [inverse_factor(): pl.pallas_call(factor_kernel, out_shape=jax.ShapeDtypeStruct((PANEL, PANE...]
    ppermute x4, waiting for transfers between devices: 0.01 us -> 27.6 us  [local(): arrived.append(lax.ppermute(sent, FRONT_AXES, pairs))]
    ppermute x4, starting transfers between devices: 15.9 us -> 35.7 us  [local(): pieces.append(lax.ppermute(schur, FRONT_AXES, pairs))]
    ppermute x21 -> x14, waiting for transfers between devices: 38.9 us -> 23.6 us  [fan_out(): received = [lax.ppermute(parts[k], axis, [numbers(k)]) for k in range(1, 8)]]
    ppermute x0 -> x10, waiting for transfers between devices: none -> 12.6 us  [the longest x3 12.3 us: local(): far = lax.ppermute(part, 'row', pairs)]
    ppermute x0 -> x10, starting transfers between devices: none -> 12.3 us  [the longest x7 9 us: local(): lax.ppermute(part, 'col', [(c, c ^ j) for c in range(8)])]
    all_gather x1, waiting for transfers between devices: 0.02 us -> 12 us  [local(): row_panel = lax.all_gather(mine, 'col')]
    ppermute x4, waiting for transfers between devices: 39.2 us -> 29.4 us  [local(): pieces.append(lax.ppermute(schur, FRONT_AXES, pairs))]
  transfers between devices with their start and end apart: 33 -> 35, of which waited for: 7 -> 10; matrix products, arithmetic and copies ran while one was open for 9% -> 6% of each run, Pallas kernels for 27% -> 9%
where the time goes in v2:
time: 282 us; the launch traced here: 281 us
  waiting for transfers between devices  129 us (46%)
  starting transfers between devices  78.9 us (28%)
  Pallas kernels  31.4 us (11%)
  between operations  14.1 us (5%)
  local copies, waits for them, and re-layouts  13.2 us (5%)
  matrix products  9.25 us (3%)
  other arithmetic  4.91 us (2%)
    ppermute x4, starting transfers between devices, local(): pieces.append(lax.ppermute(schur, FRONT_AXES, pairs))  35.7 us
    ppermute x4, waiting for transfers between devices, local(): pieces.append(lax.ppermute(schur, FRONT_AXES, pairs))  29.4 us
    ppermute x4, waiting for transfers between devices, local(): arrived.append(lax.ppermute(sent, FRONT_AXES, pairs))  27.6 us
    ppermute x14, waiting for transfers between devices, fan_out(): received = [lax.ppermute(parts[k], axis, [numbers(k)]) for k in range(1, 8)]  23.6 us
    ppermute x4, starting transfers between devices, local(): arrived.append(lax.ppermute(sent, FRONT_AXES, pairs))  19.6 us
    pallas_call x1, Pallas kernels, inverse_factor(): pl.pallas_call(factor_kernel, out_shape=jax.ShapeDtypeStruct((PANEL, PANE...  18.6 us
    all_gather x1, waiting for transfers between devices, local(): panel_top = lax.all_gather(panel_part, 'row', tiled=True)  17.9 us
    ppermute x3, waiting for transfers between devices, local(): far = lax.ppermute(part, 'row', pairs)  12.3 us
  transfers between devices with their start and end apart: 35, of which 10 were waited for; matrix products, arithmetic and copies ran while one was open for 6% of the time, Pallas kernels for 9%

profile of v2, /device:TPU:91, one launch (start us, length us, event | category | flops | bytes accessed | tf_op | source)
XLA Modules:
  0.0 280.7 jit_solution(4701477557834529862)
XLA Ops:
  6.5 1.3 fusion.8
  10.6 1.6 slice_bitcast_fusion.5
  21.1 23.6 %collective-permute-done.8 = f32[64,1024]{1,0:T(8,128)S(1)} collective-permute-done((f32[64,1024]{1,0:T(8,128)S(1)}, f32[64,1024]{1,0:T(8,128)S(1)}, u32[]{:S(2)}, u32[]{:S(2)}) %collective-permute-start.8) | collective-permute-done | bytes 262176 | tf_op jit(solution)/shard_map/panel_scatter/ppermute | solution.py:207
  44.7 1.8 bitcast_select_fusion
  48.6 10.4 %collective-permute-done.16 = f32[64,512]{1,0:T(8,128)S(1)} collective-permute-done((f32[64,512]{1,0:T(8,128)S(1)}, f32[64,512]{1,0:T(8,128)S(1)}, u32[]{:S(2)}, u32[]{:S(2)}) %collective-permute-start.16) | collective-permute-done | bytes 131104 | tf_op jit(solution)/shard_map/pivot_along_z/ppermute | solution.py:235
  60.4 1.9 collective-permute-done.17
  62.5 2.5 collective-permute-start.20
  65.1 2.8 collective-permute-start.22
  68.1 3.5 %collective-permute-start.24 = (f32[64,512]{1,0:T(8,128)S(1)}, f32[64,512]{1,0:T(8,128)S(1)}, u32[]{:S(2)}, u32[]{:S(2)}) collective-permute-start(f32[64,512]{1,0:T(8,128)S(1)} %broadcast_select_fusion.2.refs_0_), channel_id=1, source_target_pairs={{0,7},{1,6},{2,5},{3,4},{4,3},{5,2},{6,1},{7,0},{8,15},{9,14},{10,... | collective-permute-start | bytes 393224 | tf_op jit(solution)/shard_map/pivot_in_plane/ppermute | solution.py:240
  71.6 17.9 %all-gather.4.cloned.1.call-done.top_ref = f32[512,1024]{1,0:T(8,128)} async-done(((f32[64,1024]{1,0:T(8,128)}), f32[512,1024]{1,0:T(8,128)}) %all-gather.4.cloned.1.call-update) | async-done | bytes 2097168 | tf_op jit(solution)/shard_map/panel_gather/all_gather | solution.py:244
  91.8 5.8 %collective-permute-done.25 = f32[512,128]{1,0:T(8,128)S(1)} collective-permute-done((f32[512,128]{1,0:T(8,128)S(1)}, f32[512,128]{1,0:T(8,128)S(1)}, u32[]{:S(2)}, u32[]{:S(2)}) %collective-permute-start.25) | collective-permute-done | bytes 262176 | tf_op jit(solution)/shard_map/row_panel/ppermute | solution.py:268
  97.6 1.7 dynamic-slice_select_fusion
  99.5 4.4 %constant_dynamic-slice_fusion = (f32[256,1024]{1,0:T(8,128)}, f32[256,1024]{1,0:T(8,128)}, f32[256,1024]{1,0:T(8,128)}, f32[256,1024]{1,0:T(8,128)}) fusion(f32[1024,1024]{1,0:T(8,128)} %bitcast.28, s32[]{:T(128)S(6)} %select_n.105, s32[]{:T(128)S(6)} %select_n.103, s32[]{:T(128)S(6)} %select_n.101, s32[]{:T(128)S(6)} %select_n.88), kind=kLoop, calls=%fused_computation.22 | loop fusion | bytes 8388624 | tf_op jit(solution)/shard_map/rows_along_z/dynamic_slice | solution.py:251
  103.9 3.2 %collective-permute-start.31 = (f32[256,1024]{1,0:T(8,128)}, f32[256,1024]{1,0:T(8,128)}, u32[]{:S(2)}, u32[]{:S(2)}) collective-permute-start(f32[256,1024]{1,0:T(8,128)} %get-tuple-element.35), channel_id=1, source_target_pairs={{0,24},{8,56},{16,16},{24,48},{32,8},{40,40},{48,0},{56,32},{64,80... | collective-permute-start | bytes 3145736 | tf_op jit(solution)/shard_map/rows_along_z/ppermute | solution.py:257
  107.1 9.4 %collective-permute-start.29 = (f32[256,1024]{1,0:T(8,128)}, f32[256,1024]{1,0:T(8,128)}, u32[]{:S(2)}, u32[]{:S(2)}) collective-permute-start(f32[256,1024]{1,0:T(8,128)} %get-tuple-element.36), channel_id=1, source_target_pairs={{0,16},{8,48},{16,24},{24,56},{32,0},{40,32},{48,8},{56,40},{64,88... | collective-permute-start | bytes 3145736 | tf_op jit(solution)/shard_map/rows_along_z/ppermute | solution.py:257
  116.6 1.9 collective-permute-start.27
  118.5 5.0 %collective-permute-start.14 = (f32[256,1024]{1,0:T(8,128)}, f32[256,1024]{1,0:T(8,128)}, u32[]{:S(2)}, u32[]{:S(2)}) collective-permute-start(f32[256,1024]{1,0:T(8,128)} %get-tuple-element.38), channel_id=1, source_target_pairs={{0,0},{8,32},{16,8},{24,40},{32,16},{40,48},{48,24},{56,56},{64,72... | collective-permute-start | bytes 3145736 | tf_op jit(solution)/shard_map/rows_along_z/ppermute | solution.py:257
  123.5 18.6 %inverse_factor.1.inverse_ref = f32[512,512]{1,0:T(8,128)S(1)} custom-call(s32[3]{0:T(128)S(1)} %pad_add_fusion.place_ref, f32[64,512]{1,0:T(8,128)S(1)} %broadcast_select_fusion.2.refs_0_, f32[64,512]{1,0:T(8,128)S(1)} %collective-permute-done.18.refs_1_, f32[64,512]{1,0:T(8,128)S(1)} %collective-permute-done.19.refs_2_, ...), custom_call_target="tpu_custom_call" | custom-call | flops 10000000000 | bytes 2097152 | tf_op jit(solution)/shard_map/factor/inverse_factor/pallas_call | solution.py:97
  143.2 12.0 %all-gather.6.cloned.1.call-done = f32[4096,128]{1,0:T(8,128)} async-done(((f32[512,128]{1,0:T(8,128)}), f32[4096,128]{1,0:T(8,128)}) %all-gather.6.cloned.1.call-update) | async-done | bytes 2097168 | tf_op jit(solution)/shard_map/row_panel/all_gather | solution.py:270
  155.1 1.6 copy-done.2
  158.0 5.8 %solve.1 = (f32[1024,512]{1,0:T(8,128)S(1)}, f32[512,1024]{1,0:T(8,128)S(1)}) custom-call(f32[512,512]{1,0:T(8,128)S(1)} %copy-done.4, f32[512,1024]{1,0:T(8,128)S(1)} %copy-done, f32[8,512,128]{2,1,0:T(8,128)S(1)} %bitcast.25), custom_call_target="tpu_custom_call" | custom-call | flops 6000000000 | bytes 9437184 | tf_op jit(solution)/shard_map/solve/solve/pallas_call | solution.py:139
  163.8 2.3 convolution_subtract_fusion
  166.1 3.2 %collective-permute-start.32 = (f32[256,1024]{1,0:T(8,128)S(1)}, f32[256,1024]{1,0:T(8,128)S(1)}, u32[]{:S(2)}, u32[]{:S(2)}) collective-permute-start(f32[256,1024]{1,0:T(8,128)S(1)} %convolution_subtract_fusion), channel_id=1, source_target_pairs={{0,192},{8,136},{16,80},{24,24},{32,224},{40,168},{48,112},{56,56}... | collective-permute-start | bytes 3145736 | tf_op jit(solution)/shard_map/to_parent/ppermute | solution.py:288
  169.4 2.3 convolution_subtract_fusion.1
  172.4 3.3 %collective-permute-done.27 = f32[256,1024]{1,0:T(8,128)} collective-permute-done((f32[256,1024]{1,0:T(8,128)}, f32[256,1024]{1,0:T(8,128)}, u32[]{:S(2)}, u32[]{:S(2)}) %collective-permute-start.27) | collective-permute-done | bytes 1048608 | tf_op jit(solution)/shard_map/rows_along_z/ppermute | solution.py:257
  175.7 2.3 convolution_subtract_fusion.2
  178.0 20.7 %collective-permute-start.28 = (f32[256,1024]{1,0:T(8,128)S(1)}, f32[256,1024]{1,0:T(8,128)S(1)}, u32[]{:S(2)}, u32[]{:S(2)}) collective-permute-start(f32[256,1024]{1,0:T(8,128)S(1)} %convolution_subtract_fusion.2), channel_id=1, source_target_pairs={{0,64},{8,8},{16,208},{24,152},{32,96},{40,40},{48,240},{56,184},{... | collective-permute-start | bytes 3145736 | tf_op jit(solution)/shard_map/to_parent/ppermute | solution.py:288
  198.8 24.3 %collective-permute-done.14 = f32[256,1024]{1,0:T(8,128)} collective-permute-done((f32[256,1024]{1,0:T(8,128)}, f32[256,1024]{1,0:T(8,128)}, u32[]{:S(2)}, u32[]{:S(2)}) %collective-permute-start.14) | collective-permute-done | bytes 1048608 | tf_op jit(solution)/shard_map/rows_along_z/ppermute | solution.py:257
  223.1 2.3 convolution_subtract_fusion.3
  225.4 11.0 %collective-permute-start.26 = (f32[256,1024]{1,0:T(8,128)S(1)}, f32[256,1024]{1,0:T(8,128)}, u32[]{:S(2)}, u32[]{:S(2)}) collective-permute-start(f32[256,1024]{1,0:T(8,128)S(1)} %convolution_subtract_fusion.3), channel_id=1, source_target_pairs={{0,0},{8,72},{16,144},{24,216},{32,32},{40,104},{48,176},{56,248},... | collective-permute-start | bytes 3145736 | tf_op jit(solution)/shard_map/to_parent/ppermute | solution.py:288
  237.5 29.4 %collective-permute-done.26.refs_0_ = f32[256,1024]{1,0:T(8,128)} collective-permute-done((f32[256,1024]{1,0:T(8,128)S(1)}, f32[256,1024]{1,0:T(8,128)}, u32[]{:S(2)}, u32[]{:S(2)}) %collective-permute-start.26) | collective-permute-done | bytes 1048608 | tf_op jit(solution)/shard_map/to_parent/ppermute | solution.py:288
  266.9 6.9 %extend_add.1 = f32[512,2048]{1,0:T(8,128)} custom-call(s32[3]{0:T(128)} %copy-done.1, s32[4,60]{1,0:T(4,128)} %map_ref.1, f32[512,2048]{1,0:T(8,128)} %parent_ref.1, f32[256,1024]{1,0:T(8,128)} %collective-permute-done.26.refs_0_, f32[256,1024]{1,0:T(8,128)} %copy-done.7, f32[256,1024]{1,0:T(8,128)} %copy-done.6, f32[256,1024]{1,0:T(8,128)} %copy-done.5), custom_call_target="tpu_custom_call" | custom-call | flops 8388608 | bytes 12582912 | tf_op jit(solution)/shard_map/extend_add/extend_add/pallas_call | solution.py:190
  (84 shorter events, 21.7 us)
Async XLA Ops:
  6.5 83.0 %all-gather.4.cloned.1.call-start = ((), (), s32[]{:S(2)}) async-start(), calls=%async_computation | async-start | bytes 2359296 | tf_op jit(solution)/shard_map/panel_gather/all_gather | solution.py:244
  7.9 5.0 %collective-permute-start = (f32[64,512]{1,0:T(8,128)S(1)}, f32[64,512]{1,0:T(8,128)S(1)}, u32[]{:S(2)}, u32[]{:S(2)}) collective-permute-start(f32[64,512]{1,0:T(8,128)S(1)} %get-tuple-element.52), channel_id=1, source_target_pairs={{0,1},{64,65},{128,129},{192,193}} | collective-permute-start | bytes 393224 | tf_op jit(solution)/shard_map/pivot_to_columns/ppermute | solution.py:207
  8.5 5.0 %collective-permute-start.1 = (f32[64,512]{1,0:T(8,128)S(1)}, f32[64,512]{1,0:T(8,128)S(1)}, u32[]{:S(2)}, u32[]{:S(2)}) collective-permute-start(f32[64,512]{1,0:T(8,128)S(1)} %get-tuple-element.46), channel_id=1, source_target_pairs={{0,2},{64,66},{128,130},{192,194}} | collective-permute-start | bytes 393224 | tf_op jit(solution)/shard_map/pivot_to_columns/ppermute | solution.py:207
  9.2 5.0 %collective-permute-start.2 = (f32[64,512]{1,0:T(8,128)S(1)}, f32[64,512]{1,0:T(8,128)S(1)}, u32[]{:S(2)}, u32[]{:S(2)}) collective-permute-start(f32[64,512]{1,0:T(8,128)S(1)} %get-tuple-element.51), channel_id=1, source_target_pairs={{0,3},{64,67},{128,131},{192,195}} | collective-permute-start | bytes 393224 | tf_op jit(solution)/shard_map/pivot_to_columns/ppermute | solution.py:207
  9.9 5.0 %collective-permute-start.3 = (f32[64,512]{1,0:T(8,128)S(1)}, f32[64,512]{1,0:T(8,128)S(1)}, u32[]{:S(2)}, u32[]{:S(2)}) collective-permute-start(f32[64,512]{1,0:T(8,128)S(1)} %get-tuple-element.50), channel_id=1, source_target_pairs={{0,4},{64,68},{128,132},{192,196}} | collective-permute-start | bytes 393224 | tf_op jit(solution)/shard_map/pivot_to_columns/ppermute | solution.py:207
  12.2 5.6 %collective-permute-start.10 = (f32[64,1024]{1,0:T(8,128)S(1)}, f32[64,1024]{1,0:T(8,128)S(1)}, u32[]{:S(2)}, u32[]{:S(2)}) collective-permute-start(f32[64,1024]{1,0:T(8,128)S(1)} %get-tuple-element.41), channel_id=1, source_target_pairs={{0,32},{1,33},{2,34},{3,35},{4,36},{5,37},{6,38},{7,39},{64,96},{6... | collective-permute-start | bytes 786440 | tf_op jit(solution)/shard_map/panel_scatter/ppermute | solution.py:207
  12.9 6.2 %collective-permute-start.11 = (f32[64,1024]{1,0:T(8,128)S(1)}, f32[64,1024]{1,0:T(8,128)S(1)}, u32[]{:S(2)}, u32[]{:S(2)}) collective-permute-start(f32[64,1024]{1,0:T(8,128)S(1)} %get-tuple-element.40), channel_id=1, source_target_pairs={{0,40},{1,41},{2,42},{3,43},{4,44},{5,45},{6,46},{7,47},{64,104},{... | collective-permute-start | bytes 786440 | tf_op jit(solution)/shard_map/panel_scatter/ppermute | solution.py:207
  15.0 2.1 collective-permute-start.6
  15.7 5.5 %collective-permute-start.12 = (f32[64,1024]{1,0:T(8,128)S(1)}, f32[64,1024]{1,0:T(8,128)S(1)}, u32[]{:S(2)}, u32[]{:S(2)}) collective-permute-start(f32[64,1024]{1,0:T(8,128)S(1)} %get-tuple-element.45), channel_id=1, source_target_pairs={{0,48},{1,49},{2,50},{3,51},{4,52},{5,53},{6,54},{7,55},{64,112},{... | collective-permute-start | bytes 786440 | tf_op jit(solution)/shard_map/panel_scatter/ppermute | solution.py:207
  16.4 4.8 %collective-permute-start.13 = (f32[64,1024]{1,0:T(8,128)S(1)}, f32[64,1024]{1,0:T(8,128)S(1)}, u32[]{:S(2)}, u32[]{:S(2)}) collective-permute-start(f32[64,1024]{1,0:T(8,128)S(1)} %get-tuple-element.44), channel_id=1, source_target_pairs={{0,56},{1,57},{2,58},{3,59},{4,60},{5,61},{6,62},{7,63},{64,120},{... | collective-permute-start | bytes 786440 | tf_op jit(solution)/shard_map/panel_scatter/ppermute | solution.py:207
  17.1 4.1 %collective-permute-start.7 = (f32[64,1024]{1,0:T(8,128)S(1)}, f32[64,1024]{1,0:T(8,128)S(1)}, u32[]{:S(2)}, u32[]{:S(2)}) collective-permute-start(f32[64,1024]{1,0:T(8,128)S(1)} %get-tuple-element.43), channel_id=1, source_target_pairs={{0,8},{1,9},{2,10},{3,11},{4,12},{5,13},{6,14},{7,15},{64,72},{65,... | collective-permute-start | bytes 786440 | tf_op jit(solution)/shard_map/panel_scatter/ppermute | solution.py:207
  17.8 27.0 %collective-permute-start.8 = (f32[64,1024]{1,0:T(8,128)S(1)}, f32[64,1024]{1,0:T(8,128)S(1)}, u32[]{:S(2)}, u32[]{:S(2)}) collective-permute-start(f32[64,1024]{1,0:T(8,128)S(1)} %get-tuple-element.39), channel_id=1, source_target_pairs={{0,16},{1,17},{2,18},{3,19},{4,20},{5,21},{6,22},{7,23},{64,80},{6... | collective-permute-start | bytes 786440 | tf_op jit(solution)/shard_map/panel_scatter/ppermute | solution.py:207
  19.1 25.7 %collective-permute-start.9 = (f32[64,1024]{1,0:T(8,128)S(1)}, f32[64,1024]{1,0:T(8,128)S(1)}, u32[]{:S(2)}, u32[]{:S(2)}) collective-permute-start(f32[64,1024]{1,0:T(8,128)S(1)} %get-tuple-element.42), channel_id=1, source_target_pairs={{0,24},{1,25},{2,26},{3,27},{4,28},{5,29},{6,30},{7,31},{64,88},{6... | collective-permute-start | bytes 786440 | tf_op jit(solution)/shard_map/panel_scatter/ppermute | solution.py:207
  46.6 108.6 %all-gather.6.cloned.1.call-start = ((), (), s32[]{:S(2)}) async-start(), calls=%async_computation.1 | async-start | bytes 2359296 | tf_op jit(solution)/shard_map/row_panel/all_gather | solution.py:270
  47.3 11.7 %collective-permute-start.16 = (f32[64,512]{1,0:T(8,128)S(1)}, f32[64,512]{1,0:T(8,128)S(1)}, u32[]{:S(2)}, u32[]{:S(2)}) collective-permute-start(f32[64,512]{1,0:T(8,128)S(1)} %broadcast_select_fusion), channel_id=1, source_target_pairs={{0,16},{32,48},{1,17},{33,49},{2,18},{34,50},{3,19},{35,51},{4,20}... | collective-permute-start | bytes 393224 | tf_op jit(solution)/shard_map/pivot_along_z/ppermute | solution.py:235
  59.1 3.2 %collective-permute-start.17 = (f32[64,512]{1,0:T(8,128)S(1)}, f32[64,512]{1,0:T(8,128)S(1)}, u32[]{:S(2)}, u32[]{:S(2)}) collective-permute-start(f32[64,512]{1,0:T(8,128)S(1)} %broadcast_select_fusion.1), channel_id=1, source_target_pairs={{0,8},{16,24},{32,40},{48,56},{1,9},{17,25},{33,41},{49,57},{2,10}... | collective-permute-start | bytes 393224 | tf_op jit(solution)/shard_map/pivot_along_z/ppermute | solution.py:235
  62.3 5.5 %collective-permute-start.18 = (f32[64,512]{1,0:T(8,128)S(1)}, f32[64,512]{1,0:T(8,128)S(1)}, u32[]{:S(2)}, u32[]{:S(2)}) collective-permute-start(f32[64,512]{1,0:T(8,128)S(1)} %broadcast_select_fusion.2.refs_0_), channel_id=1, source_target_pairs={{0,1},{1,0},{2,3},{3,2},{4,5},{5,4},{6,7},{7,6},{8,9},{9,8},{10,11... | collective-permute-start | bytes 393224 | tf_op jit(solution)/shard_map/pivot_in_plane/ppermute | solution.py:240
  62.4 5.7 %collective-permute-start.19 = (f32[64,512]{1,0:T(8,128)S(1)}, f32[64,512]{1,0:T(8,128)S(1)}, u32[]{:S(2)}, u32[]{:S(2)}) collective-permute-start(f32[64,512]{1,0:T(8,128)S(1)} %broadcast_select_fusion.2.refs_0_), channel_id=1, source_target_pairs={{0,2},{1,3},{2,0},{3,1},{4,6},{5,7},{6,4},{7,5},{8,10},{9,11},{10,... | collective-permute-start | bytes 393224 | tf_op jit(solution)/shard_map/pivot_in_plane/ppermute | solution.py:240
  62.5 27.0 %collective-permute-start.20 = (f32[64,512]{1,0:T(8,128)S(1)}, f32[64,512]{1,0:T(8,128)S(1)}, u32[]{:S(2)}, u32[]{:S(2)}) collective-permute-start(f32[64,512]{1,0:T(8,128)S(1)} %broadcast_select_fusion.2.refs_0_), channel_id=1, source_target_pairs={{0,3},{1,2},{2,1},{3,0},{4,7},{5,6},{6,5},{7,4},{8,11},{9,10},{10,... | collective-permute-start | bytes 393224 | tf_op jit(solution)/shard_map/pivot_in_plane/ppermute | solution.py:240
  65.1 24.5 %collective-permute-start.21 = (f32[64,512]{1,0:T(8,128)S(1)}, f32[64,512]{1,0:T(8,128)S(1)}, u32[]{:S(2)}, u32[]{:S(2)}) collective-permute-start(f32[64,512]{1,0:T(8,128)S(1)} %broadcast_select_fusion.2.refs_0_), channel_id=1, source_target_pairs={{0,4},{1,5},{2,6},{3,7},{4,0},{5,1},{6,2},{7,3},{8,12},{9,13},{10,... | collective-permute-start | bytes 393224 | tf_op jit(solution)/shard_map/pivot_in_plane/ppermute | solution.py:240
  65.1 24.5 %collective-permute-start.22 = (f32[64,512]{1,0:T(8,128)S(1)}, f32[64,512]{1,0:T(8,128)S(1)}, u32[]{:S(2)}, u32[]{:S(2)}) collective-permute-start(f32[64,512]{1,0:T(8,128)S(1)} %broadcast_select_fusion.2.refs_0_), channel_id=1, source_target_pairs={{0,5},{1,4},{2,7},{3,6},{4,1},{5,0},{6,3},{7,2},{8,13},{9,12},{10,... | collective-permute-start | bytes 393224 | tf_op jit(solution)/shard_map/pivot_in_plane/ppermute | solution.py:240
  67.8 21.7 %collective-permute-start.23 = (f32[64,512]{1,0:T(8,128)S(1)}, f32[64,512]{1,0:T(8,128)S(1)}, u32[]{:S(2)}, u32[]{:S(2)}) collective-permute-start(f32[64,512]{1,0:T(8,128)S(1)} %broadcast_select_fusion.2.refs_0_), channel_id=1, source_target_pairs={{0,6},{1,7},{2,4},{3,5},{4,2},{5,3},{6,0},{7,1},{8,14},{9,15},{10,... | collective-permute-start | bytes 393224 | tf_op jit(solution)/shard_map/pivot_in_plane/ppermute | solution.py:240
  68.1 21.4 %collective-permute-start.24 = (f32[64,512]{1,0:T(8,128)S(1)}, f32[64,512]{1,0:T(8,128)S(1)}, u32[]{:S(2)}, u32[]{:S(2)}) collective-permute-start(f32[64,512]{1,0:T(8,128)S(1)} %broadcast_select_fusion.2.refs_0_), channel_id=1, source_target_pairs={{0,7},{1,6},{2,5},{3,4},{4,3},{5,2},{6,1},{7,0},{8,15},{9,14},{10,... | collective-permute-start | bytes 393224 | tf_op jit(solution)/shard_map/pivot_in_plane/ppermute | solution.py:240
  90.5 7.1 %collective-permute-start.25 = (f32[512,128]{1,0:T(8,128)S(1)}, f32[512,128]{1,0:T(8,128)S(1)}, u32[]{:S(2)}, u32[]{:S(2)}) collective-permute-start(f32[512,128]{1,0:T(8,128)S(1)} %constant_dynamic-slice_fusion.3), channel_id=1, source_target_pairs={{0,1},{2,3},{4,5},{6,7},{8,9},{10,11},{12,13},{14,15},{16,17},{18,... | collective-permute-start | bytes 786440 | tf_op jit(solution)/shard_map/row_panel/ppermute | solution.py:268
  103.9 59.9 %collective-permute-start.31 = (f32[256,1024]{1,0:T(8,128)}, f32[256,1024]{1,0:T(8,128)}, u32[]{:S(2)}, u32[]{:S(2)}) collective-permute-start(f32[256,1024]{1,0:T(8,128)} %get-tuple-element.35), channel_id=1, source_target_pairs={{0,24},{8,56},{16,16},{24,48},{32,8},{40,40},{48,0},{56,32},{64,80... | collective-permute-start | bytes 3145736 | tf_op jit(solution)/shard_map/rows_along_z/ppermute | solution.py:257
  107.1 62.2 %collective-permute-start.29 = (f32[256,1024]{1,0:T(8,128)}, f32[256,1024]{1,0:T(8,128)}, u32[]{:S(2)}, u32[]{:S(2)}) collective-permute-start(f32[256,1024]{1,0:T(8,128)} %get-tuple-element.36), channel_id=1, source_target_pairs={{0,16},{8,48},{16,24},{24,56},{32,0},{40,32},{48,8},{56,40},{64,88... | collective-permute-start | bytes 3145736 | tf_op jit(solution)/shard_map/rows_along_z/ppermute | solution.py:257
  116.6 59.1 %collective-permute-start.27 = (f32[256,1024]{1,0:T(8,128)}, f32[256,1024]{1,0:T(8,128)}, u32[]{:S(2)}, u32[]{:S(2)}) collective-permute-start(f32[256,1024]{1,0:T(8,128)} %get-tuple-element.37), channel_id=1, source_target_pairs={{0,8},{8,40},{16,0},{24,32},{32,24},{40,56},{48,16},{56,48},{64,64... | collective-permute-start | bytes 3145736 | tf_op jit(solution)/shard_map/rows_along_z/ppermute | solution.py:257
  118.5 104.6 %collective-permute-start.14 = (f32[256,1024]{1,0:T(8,128)}, f32[256,1024]{1,0:T(8,128)}, u32[]{:S(2)}, u32[]{:S(2)}) collective-permute-start(f32[256,1024]{1,0:T(8,128)} %get-tuple-element.38), channel_id=1, source_target_pairs={{0,0},{8,32},{16,8},{24,40},{32,16},{40,48},{48,24},{56,56},{64,72... | collective-permute-start | bytes 3145736 | tf_op jit(solution)/shard_map/rows_along_z/ppermute | solution.py:257
  166.1 70.3 %collective-permute-start.32 = (f32[256,1024]{1,0:T(8,128)S(1)}, f32[256,1024]{1,0:T(8,128)S(1)}, u32[]{:S(2)}, u32[]{:S(2)}) collective-permute-start(f32[256,1024]{1,0:T(8,128)S(1)} %convolution_subtract_fusion), channel_id=1, source_target_pairs={{0,192},{8,136},{16,80},{24,24},{32,224},{40,168},{48,112},{56,56}... | collective-permute-start | bytes 3145736 | tf_op jit(solution)/shard_map/to_parent/ppermute | solution.py:288
  171.7 64.8 %collective-permute-start.30 = (f32[256,1024]{1,0:T(8,128)S(1)}, f32[256,1024]{1,0:T(8,128)S(1)}, u32[]{:S(2)}, u32[]{:S(2)}) collective-permute-start(f32[256,1024]{1,0:T(8,128)S(1)} %convolution_subtract_fusion.1), channel_id=1, source_target_pairs={{0,128},{8,200},{16,16},{24,88},{32,160},{40,232},{48,48},{56,120}... | collective-permute-start | bytes 3145736 | tf_op jit(solution)/shard_map/to_parent/ppermute | solution.py:288
  178.0 58.5 %collective-permute-start.28 = (f32[256,1024]{1,0:T(8,128)S(1)}, f32[256,1024]{1,0:T(8,128)S(1)}, u32[]{:S(2)}, u32[]{:S(2)}) collective-permute-start(f32[256,1024]{1,0:T(8,128)S(1)} %convolution_subtract_fusion.2), channel_id=1, source_target_pairs={{0,64},{8,8},{16,208},{24,152},{32,96},{40,40},{48,240},{56,184},{... | collective-permute-start | bytes 3145736 | tf_op jit(solution)/shard_map/to_parent/ppermute | solution.py:288
  225.4 41.5 %collective-permute-start.26 = (f32[256,1024]{1,0:T(8,128)S(1)}, f32[256,1024]{1,0:T(8,128)}, u32[]{:S(2)}, u32[]{:S(2)}) collective-permute-start(f32[256,1024]{1,0:T(8,128)S(1)} %convolution_subtract_fusion.3), channel_id=1, source_target_pairs={{0,0},{8,72},{16,144},{24,216},{32,32},{40,104},{48,176},{56,248},... | collective-permute-start | bytes 3145736 | tf_op jit(solution)/shard_map/to_parent/ppermute | solution.py:288
  (16 other events, 152.0 us)
Sparse Core Ops, SparseCore 0:
  46.7 42.7 all-gather.3
  99.5 55.6 all-gather.5

commit v3 on v2

--- a/solution.py
+++ b/solution.py
@@ -71,13 +71,8 @@
     )
 
 
-def factor_kernel(place_ref, *refs):
-    parts, out_ref, work = refs[:8], refs[8], refs[9]
-    my_col = place_ref[2]
-    chunk = PANEL // 8
-    for j in range(8):
-        start = pl.multiple_of(chunk * (my_col ^ j), chunk)
-        work[pl.ds(start, chunk), :] = parts[j][...]
+def factor_kernel(pivot_ref, out_ref, work):
+    work[...] = pivot_ref[...]
     for k in range(PANEL // TILE):
         low, high = k * TILE, (k + 1) * TILE
         inverse = eliminate(work[low:high, low:high])
@@ -93,20 +88,19 @@
     out_ref[...] = work[...]
 
 
-def inverse_factor(place, parts):
+def inverse_factor(pivot_block):
     return pl.pallas_call(
         factor_kernel,
         out_shape=jax.ShapeDtypeStruct((PANEL, PANEL), jnp.float32),
-        in_specs=[pl.BlockSpec(memory_space=pltpu.SMEM)]
-        + [pl.BlockSpec(memory_space=pltpu.VMEM)] * 8,
+        in_specs=[pl.BlockSpec(memory_space=pltpu.VMEM)],
         out_specs=pl.BlockSpec(memory_space=pltpu.VMEM),
         scratch_shapes=[pltpu.VMEM((PANEL, PANEL), jnp.float32)],
         compiler_params=pltpu.CompilerParams(vmem_limit_bytes=24 * 2**20),
         cost_estimate=pl.CostEstimate(
-            flops=10_000_000_000, bytes_accessed=2 * 2**20, transcendentals=0
+            flops=300_000_000, bytes_accessed=2 * 2**20, transcendentals=0
         ),
         name="inverse_factor",
-    )(place, *parts)
+    )(pivot_block)
 
 
 def split(value):
@@ -146,7 +140,7 @@
         out_specs=(vmem, vmem),
         compiler_params=pltpu.CompilerParams(vmem_limit_bytes=40 * 2**20),
         cost_estimate=pl.CostEstimate(
-            flops=6_000_000_000, bytes_accessed=9 * 2**20, transcendentals=0
+            flops=3_000_000_000, bytes_accessed=9 * 2**20, transcendentals=0
         ),
         name="solve",
     )(inverse, panel_top, row_panel)
@@ -227,7 +221,6 @@
         parts = [matrix[chunk * k : chunk * (k + 1), :] for k in range(8)]
         panel_part = fan_out(parts, "row", lambda k: (0, k))
         panel_part = jnp.where(my_row == 0, parts[0], panel_part)
-        part, panel_part = lax.optimization_barrier((part, panel_part))
 
     with jax.named_scope("pivot_along_z"):
         for distance in (4, 2, 1):
@@ -236,9 +229,7 @@
             part = jnp.where((my_row & (2 * distance - 1)) == distance, far, part)
 
     with jax.named_scope("pivot_in_plane"):
-        parts = [part] + [
-            lax.ppermute(part, "col", [(c, c ^ j) for c in range(8)]) for j in range(1, 8)
-        ]
+        pivot_block = lax.all_gather(part, "col", tiled=True)
 
     with jax.named_scope("panel_gather"):
         panel_top = lax.all_gather(panel_part, "row", tiled=True)
@@ -257,7 +248,6 @@
             arrived.append(lax.ppermute(sent, FRONT_AXES, pairs))
 
     with jax.named_scope("row_panel"):
-        panel_top, *parts = lax.optimization_barrier((panel_top, *parts))
         half = my_col & 1
         start = PIECE * quarter
         mine = lax.dynamic_slice_in_dim(panel_top, start + TILE * half, TILE, 1)
@@ -270,7 +260,7 @@
         row_panel = lax.all_gather(mine, "col")
 
     with jax.named_scope("factor"):
-        inverse = inverse_factor(place, parts)
+        inverse = inverse_factor(pivot_block)
 
     with jax.named_scope("solve"):
         lower, upper = solve(inverse, panel_top, row_panel)

time: 282 us -> 275 us (0.975)
  starting transfers between devices: 78.9 us -> 48.4 us
  waiting for transfers between devices: 129 us -> 154 us
    all_gather x1, waiting for transfers between devices: 12 us -> 37.3 us  [local(): row_panel = lax.all_gather(mine, 'col')]
    ppermute x3, waiting for transfers between devices: 12.3 us -> 37.1 us  [local(): far = lax.ppermute(part, 'row', pairs)]
    ppermute x4, starting transfers between devices: 35.7 us -> 17.6 us  [local(): pieces.append(lax.ppermute(schur, FRONT_AXES, pairs))]
    ppermute x14, waiting for transfers between devices: 23.6 us -> 9.53 us  [fan_out(): received = [lax.ppermute(parts[k], axis, [numbers(k)]) for k in range(1, 8)]]
    ppermute x4, waiting for transfers between devices: 27.6 us -> 16.5 us  [local(): arrived.append(lax.ppermute(sent, FRONT_AXES, pairs))]
    all_gather x1, waiting for transfers between devices: 17.9 us -> 6.98 us  [local(): panel_top = lax.all_gather(panel_part, 'row', tiled=True)]
    all_gather x0 -> x1, waiting for transfers between devices: none -> 9.99 us  [local(): pivot_block = lax.all_gather(part, 'col', tiled=True)]
    ppermute x7 -> x0, starting transfers between devices: 9 us -> none  [local(): lax.ppermute(part, 'col', [(c, c ^ j) for c in range(8)])]
  transfers between devices with their start and end apart: 35 -> 29, of which waited for: 10 -> 9; matrix products, arithmetic and copies ran while one was open for 6% -> 7% of each run, Pallas kernels for 9% -> 9%
where the time goes in v3:
time: 275 us; the launch traced here: 273 us
  waiting for transfers between devices  154 us (56%)
  starting transfers between devices  48.4 us (18%)
  Pallas kernels  30.8 us (11%)
  between operations  13.7 us (5%)
  local copies, waits for them, and re-layouts  11.3 us (4%)
  matrix products  9.37 us (3%)
  other arithmetic  5.85 us (2%)
    all_gather x1, waiting for transfers between devices, local(): row_panel = lax.all_gather(mine, 'col')  37.3 us
    ppermute x3, waiting for transfers between devices, local(): far = lax.ppermute(part, 'row', pairs)  37.1 us
    ppermute x4, waiting for transfers between devices, local(): pieces.append(lax.ppermute(schur, FRONT_AXES, pairs))  29.8 us
    pallas_call x1, Pallas kernels, inverse_factor(): pl.pallas_call(factor_kernel, out_shape=jax.ShapeDtypeStruct((PANEL, PANE...  18 us
    ppermute x4, starting transfers between devices, local(): pieces.append(lax.ppermute(schur, FRONT_AXES, pairs))  17.6 us
    ppermute x4, waiting for transfers between devices, local(): arrived.append(lax.ppermute(sent, FRONT_AXES, pairs))  16.5 us
    ppermute x4, starting transfers between devices, local(): arrived.append(lax.ppermute(sent, FRONT_AXES, pairs))  16.2 us
    ppermute x14, starting transfers between devices, fan_out(): received = [lax.ppermute(parts[k], axis, [numbers(k)]) for k in range(1, 8)]  10 us
  transfers between devices with their start and end apart: 29, of which 9 were waited for; matrix products, arithmetic and copies ran while one was open for 7% of the time, Pallas kernels for 9%

profile of v3, /device:TPU:91, one launch (start us, length us, event | category | flops | bytes accessed | tf_op | source)
XLA Modules:
  0.0 273.1 jit_solution(13771753203575444552)
XLA Ops:
  6.5 1.6 slice_bitcast_fusion.5
  8.8 1.3 collective-permute-start.1
  12.9 9.5 %collective-permute-done.1 = f32[64,1024]{1,0:T(8,128)S(1)} collective-permute-done((f32[64,1024]{1,0:T(8,128)S(1)}, f32[64,1024]{1,0:T(8,128)S(1)}, u32[]{:S(2)}, u32[]{:S(2)}) %collective-permute-start.1) | collective-permute-done | bytes 262176 | tf_op jit(solution)/shard_map/panel_scatter/ppermute | solution.py:201
  23.1 1.8 bitcast_select_fusion
  25.0 1.3 fusion.8
  32.8 1.3 collective-permute-start.16
  34.1 32.7 %collective-permute-done.16 = f32[64,512]{1,0:T(8,128)S(1)} collective-permute-done((f32[64,512]{1,0:T(8,128)S(1)}, f32[64,512]{1,0:T(8,128)S(1)}, u32[]{:S(2)}, u32[]{:S(2)}) %collective-permute-start.16) | collective-permute-done | bytes 131104 | tf_op jit(solution)/shard_map/pivot_along_z/ppermute | solution.py:228
  66.8 1.3 collective-permute-start.17
  68.1 4.4 %collective-permute-done.17 = f32[64,512]{1,0:T(8,128)S(1)} collective-permute-done((f32[64,512]{1,0:T(8,128)S(1)}, f32[64,512]{1,0:T(8,128)S(1)}, u32[]{:S(2)}, u32[]{:S(2)}) %collective-permute-start.17) | collective-permute-done | bytes 131104 | tf_op jit(solution)/shard_map/pivot_along_z/ppermute | solution.py:228
  73.3 7.0 %all-gather.5.cloned.1.call-done.top_ref = f32[512,1024]{1,0:T(8,128)} async-done(((f32[64,1024]{1,0:T(8,128)}), f32[512,1024]{1,0:T(8,128)}) %all-gather.5.cloned.1.call-update) | async-done | bytes 2097168 | tf_op jit(solution)/shard_map/panel_gather/all_gather | solution.py:235
  82.6 6.5 %collective-permute-done.18 = f32[512,128]{1,0:T(8,128)S(1)} collective-permute-done((f32[512,128]{1,0:T(8,128)S(1)}, f32[512,128]{1,0:T(8,128)S(1)}, u32[]{:S(2)}, u32[]{:S(2)}) %collective-permute-start.18) | collective-permute-done | bytes 262176 | tf_op jit(solution)/shard_map/row_panel/ppermute | solution.py:258
  89.1 1.7 dynamic-slice_select_fusion
  90.9 4.5 %constant_dynamic-slice_fusion = (f32[256,1024]{1,0:T(8,128)}, f32[256,1024]{1,0:T(8,128)}, f32[256,1024]{1,0:T(8,128)}, f32[256,1024]{1,0:T(8,128)}) fusion(f32[1024,1024]{1,0:T(8,128)} %bitcast.28, s32[]{:T(128)S(6)} %select_n.105, s32[]{:T(128)S(6)} %select_n.103, s32[]{:T(128)S(6)} %select_n.101, s32[]{:T(128)S(6)} %select_n.86), kind=kLoop, calls=%fused_computation.22 | loop fusion | bytes 8388624 | tf_op jit(solution)/shard_map/rows_along_z/dynamic_slice | solution.py:242
  95.4 1.9 collective-permute-start.24
  97.3 9.5 %collective-permute-start.22 = (f32[256,1024]{1,0:T(8,128)}, f32[256,1024]{1,0:T(8,128)}, u32[]{:S(2)}, u32[]{:S(2)}) collective-permute-start(f32[256,1024]{1,0:T(8,128)} %get-tuple-element.14), channel_id=1, source_target_pairs={{0,16},{8,48},{16,24},{24,56},{32,0},{40,32},{48,8},{56,40},{64,88... | collective-permute-start | bytes 3145736 | tf_op jit(solution)/shard_map/rows_along_z/ppermute | solution.py:248
  106.8 2.1 collective-permute-start.20
  108.9 10.0 %all-gather.7.cloned.1.call-done.pivot_ref = f32[512,512]{1,0:T(8,128)} async-done(((f32[64,512]{1,0:T(8,128)}), f32[512,512]{1,0:T(8,128)}) %all-gather.7.cloned.1.call-update) | async-done | bytes 1048592 | tf_op jit(solution)/shard_map/pivot_in_plane/all_gather | solution.py:232
  120.1 18.0 %inverse_factor.1.inverse_ref = f32[512,512]{1,0:T(8,128)S(1)} custom-call(f32[512,512]{1,0:T(8,128)S(1)} %copy-done), custom_call_target="tpu_custom_call" | custom-call | flops 300000000 | bytes 2097152 | tf_op jit(solution)/shard_map/factor/inverse_factor/pallas_call | solution.py:92
  138.2 2.7 %collective-permute-start.7 = (f32[256,1024]{1,0:T(8,128)}, f32[256,1024]{1,0:T(8,128)}, u32[]{:S(2)}, u32[]{:S(2)}) collective-permute-start(f32[256,1024]{1,0:T(8,128)} %get-tuple-element.16), channel_id=1, source_target_pairs={{0,0},{8,32},{16,8},{24,40},{32,16},{40,48},{48,24},{56,56},{64,72... | collective-permute-start | bytes 3145736 | tf_op jit(solution)/shard_map/rows_along_z/ppermute | solution.py:248
  140.9 37.3 %all-gather.9.cloned.1.call-done = f32[4096,128]{1,0:T(8,128)} async-done(((f32[512,128]{1,0:T(8,128)}), f32[4096,128]{1,0:T(8,128)}) %all-gather.9.cloned.1.call-update) | async-done | bytes 2097168 | tf_op jit(solution)/shard_map/row_panel/all_gather | solution.py:260
  178.2 1.6 copy-done.2
  179.8 5.8 %solve.1 = (f32[1024,512]{1,0:T(8,128)S(1)}, f32[512,1024]{1,0:T(8,128)S(1)}) custom-call(f32[512,512]{1,0:T(8,128)S(1)} %inverse_factor.1.inverse_ref, f32[512,1024]{1,0:T(8,128)S(1)} %copy-done.1, f32[8,512,128]{2,1,0:T(8,128)S(1)} %bitcast.25), custom_call_target="tpu_custom_call" | custom-call | flops 3000000000 | bytes 9437184 | tf_op jit(solution)/shard_map/solve/solve/pallas_call | solution.py:133
  185.7 2.3 convolution_subtract_fusion
  188.0 3.0 %collective-permute-start.25 = (f32[256,1024]{1,0:T(8,128)S(1)}, f32[256,1024]{1,0:T(8,128)S(1)}, u32[]{:S(2)}, u32[]{:S(2)}) collective-permute-start(f32[256,1024]{1,0:T(8,128)S(1)} %convolution_subtract_fusion), channel_id=1, source_target_pairs={{0,192},{8,136},{16,80},{24,24},{32,224},{40,168},{48,112},{56,56}... | collective-permute-start | bytes 3145736 | tf_op jit(solution)/shard_map/to_parent/ppermute | solution.py:278
  191.0 2.4 convolution_subtract_fusion.1
  194.1 2.3 convolution_subtract_fusion.2
  196.5 3.7 %collective-permute-start.21 = (f32[256,1024]{1,0:T(8,128)S(1)}, f32[256,1024]{1,0:T(8,128)S(1)}, u32[]{:S(2)}, u32[]{:S(2)}) collective-permute-start(f32[256,1024]{1,0:T(8,128)S(1)} %convolution_subtract_fusion.2), channel_id=1, source_target_pairs={{0,64},{8,8},{16,208},{24,152},{32,96},{40,40},{48,240},{56,184},{... | collective-permute-start | bytes 3145736 | tf_op jit(solution)/shard_map/to_parent/ppermute | solution.py:278
  200.2 16.5 %collective-permute-done.7 = f32[256,1024]{1,0:T(8,128)} collective-permute-done((f32[256,1024]{1,0:T(8,128)}, f32[256,1024]{1,0:T(8,128)}, u32[]{:S(2)}, u32[]{:S(2)}) %collective-permute-start.7) | collective-permute-done | bytes 1048608 | tf_op jit(solution)/shard_map/rows_along_z/ppermute | solution.py:248
  216.7 2.3 convolution_subtract_fusion.3
  219.0 10.1 %collective-permute-start.19 = (f32[256,1024]{1,0:T(8,128)S(1)}, f32[256,1024]{1,0:T(8,128)}, u32[]{:S(2)}, u32[]{:S(2)}) collective-permute-start(f32[256,1024]{1,0:T(8,128)S(1)} %convolution_subtract_fusion.3), channel_id=1, source_target_pairs={{0,0},{8,72},{16,144},{24,216},{32,32},{40,104},{48,176},{56,248},... | collective-permute-start | bytes 3145736 | tf_op jit(solution)/shard_map/to_parent/ppermute | solution.py:278
  229.9 29.7 %collective-permute-done.19.refs_0_ = f32[256,1024]{1,0:T(8,128)} collective-permute-done((f32[256,1024]{1,0:T(8,128)S(1)}, f32[256,1024]{1,0:T(8,128)}, u32[]{:S(2)}, u32[]{:S(2)}) %collective-permute-start.19) | collective-permute-done | bytes 1048608 | tf_op jit(solution)/shard_map/to_parent/ppermute | solution.py:278
  259.6 6.9 %extend_add.1 = f32[512,2048]{1,0:T(8,128)} custom-call(s32[3]{0:T(128)} %pad_add_fusion.place_ref, s32[4,60]{1,0:T(4,128)} %map_ref.1, f32[512,2048]{1,0:T(8,128)} %parent_ref.1, f32[256,1024]{1,0:T(8,128)} %collective-permute-done.19.refs_0_, f32[256,1024]{1,0:T(8,128)} %copy-done.5, f32[256,1024]{1,0:T(8,128)} %copy-done.4, f32[256,1024]{1,0:T(8,128)} %copy-done.3), custom_call_target="tpu_custom_call" | custom-call | flops 8388608 | bytes 12582912 | tf_op jit(solution)/shard_map/extend_add/extend_add/pallas_call | solution.py:184
  (59 shorter events, 16.2 us)
Async XLA Ops:
  6.5 73.7 %all-gather.5.cloned.1.call-start = ((), (), s32[]{:S(2)}) async-start(), calls=%async_computation | async-start | bytes 2359296 | tf_op jit(solution)/shard_map/panel_gather/all_gather | solution.py:235
  8.1 4.0 %collective-permute-start = (f32[64,1024]{1,0:T(8,128)S(1)}, f32[64,1024]{1,0:T(8,128)S(1)}, u32[]{:S(2)}, u32[]{:S(2)}) collective-permute-start(f32[64,1024]{1,0:T(8,128)S(1)} %get-tuple-element.29), channel_id=1, source_target_pairs={{0,8},{1,9},{2,10},{3,11},{4,12},{5,13},{6,14},{7,15},{64,72},{65,... | collective-permute-start | bytes 786440 | tf_op jit(solution)/shard_map/panel_scatter/ppermute | solution.py:201
  8.8 13.5 %collective-permute-start.1 = (f32[64,1024]{1,0:T(8,128)S(1)}, f32[64,1024]{1,0:T(8,128)S(1)}, u32[]{:S(2)}, u32[]{:S(2)}) collective-permute-start(f32[64,1024]{1,0:T(8,128)S(1)} %get-tuple-element.24), channel_id=1, source_target_pairs={{0,16},{1,17},{2,18},{3,19},{4,20},{5,21},{6,22},{7,23},{64,80},{6... | collective-permute-start | bytes 786440 | tf_op jit(solution)/shard_map/panel_scatter/ppermute | solution.py:201
  10.1 12.9 %collective-permute-start.2 = (f32[64,1024]{1,0:T(8,128)S(1)}, f32[64,1024]{1,0:T(8,128)S(1)}, u32[]{:S(2)}, u32[]{:S(2)}) collective-permute-start(f32[64,1024]{1,0:T(8,128)S(1)} %get-tuple-element.28), channel_id=1, source_target_pairs={{0,24},{1,25},{2,26},{3,27},{4,28},{5,29},{6,30},{7,31},{64,88},{6... | collective-permute-start | bytes 786440 | tf_op jit(solution)/shard_map/panel_scatter/ppermute | solution.py:201
  10.8 12.3 %collective-permute-start.3 = (f32[64,1024]{1,0:T(8,128)S(1)}, f32[64,1024]{1,0:T(8,128)S(1)}, u32[]{:S(2)}, u32[]{:S(2)}) collective-permute-start(f32[64,1024]{1,0:T(8,128)S(1)} %get-tuple-element.27), channel_id=1, source_target_pairs={{0,32},{1,33},{2,34},{3,35},{4,36},{5,37},{6,38},{7,39},{64,96},{6... | collective-permute-start | bytes 786440 | tf_op jit(solution)/shard_map/panel_scatter/ppermute | solution.py:201
  11.5 11.6 %collective-permute-start.4 = (f32[64,1024]{1,0:T(8,128)S(1)}, f32[64,1024]{1,0:T(8,128)S(1)}, u32[]{:S(2)}, u32[]{:S(2)}) collective-permute-start(f32[64,1024]{1,0:T(8,128)S(1)} %get-tuple-element.26), channel_id=1, source_target_pairs={{0,40},{1,41},{2,42},{3,43},{4,44},{5,45},{6,46},{7,47},{64,104},{... | collective-permute-start | bytes 786440 | tf_op jit(solution)/shard_map/panel_scatter/ppermute | solution.py:201
  12.2 10.9 %collective-permute-start.5 = (f32[64,1024]{1,0:T(8,128)S(1)}, f32[64,1024]{1,0:T(8,128)S(1)}, u32[]{:S(2)}, u32[]{:S(2)}) collective-permute-start(f32[64,1024]{1,0:T(8,128)S(1)} %get-tuple-element.25), channel_id=1, source_target_pairs={{0,48},{1,49},{2,50},{3,51},{4,52},{5,53},{6,54},{7,55},{64,112},{... | collective-permute-start | bytes 786440 | tf_op jit(solution)/shard_map/panel_scatter/ppermute | solution.py:201
  22.4 0.7 collective-permute-start.6
  24.9 94.0 %all-gather.7.cloned.1.call-start = ((), (), s32[]{:S(2)}) async-start(), calls=%async_computation.1 | async-start | bytes 1179648 | tf_op jit(solution)/shard_map/pivot_in_plane/all_gather | solution.py:232
  26.3 3.4 %collective-permute-start.10 = (f32[64,512]{1,0:T(8,128)S(1)}, f32[64,512]{1,0:T(8,128)S(1)}, u32[]{:S(2)}, u32[]{:S(2)}) collective-permute-start(f32[64,512]{1,0:T(8,128)S(1)} %get-tuple-element.22), channel_id=1, source_target_pairs={{0,3},{64,67},{128,131},{192,195}} | collective-permute-start | bytes 393224 | tf_op jit(solution)/shard_map/pivot_to_columns/ppermute | solution.py:201
  27.0 3.4 %collective-permute-start.11 = (f32[64,512]{1,0:T(8,128)S(1)}, f32[64,512]{1,0:T(8,128)S(1)}, u32[]{:S(2)}, u32[]{:S(2)}) collective-permute-start(f32[64,512]{1,0:T(8,128)S(1)} %get-tuple-element.21), channel_id=1, source_target_pairs={{0,4},{64,68},{128,132},{192,196}} | collective-permute-start | bytes 393224 | tf_op jit(solution)/shard_map/pivot_to_columns/ppermute | solution.py:201
  27.6 3.4 %collective-permute-start.12 = (f32[64,512]{1,0:T(8,128)S(1)}, f32[64,512]{1,0:T(8,128)S(1)}, u32[]{:S(2)}, u32[]{:S(2)}) collective-permute-start(f32[64,512]{1,0:T(8,128)S(1)} %get-tuple-element.20), channel_id=1, source_target_pairs={{0,5},{64,69},{128,133},{192,197}} | collective-permute-start | bytes 393224 | tf_op jit(solution)/shard_map/pivot_to_columns/ppermute | solution.py:201
  28.3 2.7 %collective-permute-start.13 = (f32[64,512]{1,0:T(8,128)S(1)}, f32[64,512]{1,0:T(8,128)S(1)}, u32[]{:S(2)}, u32[]{:S(2)}) collective-permute-start(f32[64,512]{1,0:T(8,128)S(1)} %get-tuple-element.19), channel_id=1, source_target_pairs={{0,6},{64,70},{128,134},{192,198}} | collective-permute-start | bytes 393224 | tf_op jit(solution)/shard_map/pivot_to_columns/ppermute | solution.py:201
  29.0 2.1 collective-permute-start.14
  29.7 1.4 collective-permute-start.8
  30.4 0.7 collective-permute-start.9
  32.1 0.7 collective-permute-start.15
  32.8 34.0 %collective-permute-start.16 = (f32[64,512]{1,0:T(8,128)S(1)}, f32[64,512]{1,0:T(8,128)S(1)}, u32[]{:S(2)}, u32[]{:S(2)}) collective-permute-start(f32[64,512]{1,0:T(8,128)S(1)} %broadcast_select_fusion), channel_id=1, source_target_pairs={{0,16},{32,48},{1,17},{33,49},{2,18},{34,50},{3,19},{35,51},{4,20}... | collective-permute-start | bytes 393224 | tf_op jit(solution)/shard_map/pivot_along_z/ppermute | solution.py:228
  66.8 5.7 %collective-permute-start.17 = (f32[64,512]{1,0:T(8,128)S(1)}, f32[64,512]{1,0:T(8,128)S(1)}, u32[]{:S(2)}, u32[]{:S(2)}) collective-permute-start(f32[64,512]{1,0:T(8,128)S(1)} %broadcast_select_fusion.1), channel_id=1, source_target_pairs={{0,8},{16,24},{32,40},{48,56},{1,9},{17,25},{33,41},{49,57},{2,10}... | collective-permute-start | bytes 393224 | tf_op jit(solution)/shard_map/pivot_along_z/ppermute | solution.py:228
  73.2 105.0 %all-gather.9.cloned.1.call-start = ((), (), s32[]{:S(2)}) async-start(), calls=%async_computation.2 | async-start | bytes 2359296 | tf_op jit(solution)/shard_map/row_panel/all_gather | solution.py:260
  81.2 7.9 %collective-permute-start.18 = (f32[512,128]{1,0:T(8,128)S(1)}, f32[512,128]{1,0:T(8,128)S(1)}, u32[]{:S(2)}, u32[]{:S(2)}) collective-permute-start(f32[512,128]{1,0:T(8,128)S(1)} %constant_dynamic-slice_fusion.3), channel_id=1, source_target_pairs={{0,1},{2,3},{4,5},{6,7},{8,9},{10,11},{12,13},{14,15},{16,17},{18,... | collective-permute-start | bytes 786440 | tf_op jit(solution)/shard_map/row_panel/ppermute | solution.py:258
  90.8 87.4 %copy-start.1 = (f32[512,1024]{1,0:T(8,128)S(1)}, f32[512,1024]{1,0:T(8,128)}, u32[]{:S(2)}) copy-start(f32[512,1024]{1,0:T(8,128)} %all-gather.5.cloned.1.call-done.top_ref) | copy-start | bytes 6291460
  95.4 90.3 %collective-permute-start.24 = (f32[256,1024]{1,0:T(8,128)}, f32[256,1024]{1,0:T(8,128)}, u32[]{:S(2)}, u32[]{:S(2)}) collective-permute-start(f32[256,1024]{1,0:T(8,128)} %get-tuple-element.13), channel_id=1, source_target_pairs={{0,24},{8,56},{16,16},{24,48},{32,8},{40,40},{48,0},{56,32},{64,80... | collective-permute-start | bytes 3145736 | tf_op jit(solution)/shard_map/rows_along_z/ppermute | solution.py:248
  97.3 93.7 %collective-permute-start.22 = (f32[256,1024]{1,0:T(8,128)}, f32[256,1024]{1,0:T(8,128)}, u32[]{:S(2)}, u32[]{:S(2)}) collective-permute-start(f32[256,1024]{1,0:T(8,128)} %get-tuple-element.14), channel_id=1, source_target_pairs={{0,16},{8,48},{16,24},{24,56},{32,0},{40,32},{48,8},{56,40},{64,88... | collective-permute-start | bytes 3145736 | tf_op jit(solution)/shard_map/rows_along_z/ppermute | solution.py:248
  106.8 87.4 %collective-permute-start.20 = (f32[256,1024]{1,0:T(8,128)}, f32[256,1024]{1,0:T(8,128)}, u32[]{:S(2)}, u32[]{:S(2)}) collective-permute-start(f32[256,1024]{1,0:T(8,128)} %get-tuple-element.15), channel_id=1, source_target_pairs={{0,8},{8,40},{16,0},{24,32},{32,24},{40,56},{48,16},{56,48},{64,64... | collective-permute-start | bytes 3145736 | tf_op jit(solution)/shard_map/rows_along_z/ppermute | solution.py:248
  138.2 78.5 %collective-permute-start.7 = (f32[256,1024]{1,0:T(8,128)}, f32[256,1024]{1,0:T(8,128)}, u32[]{:S(2)}, u32[]{:S(2)}) collective-permute-start(f32[256,1024]{1,0:T(8,128)} %get-tuple-element.16), channel_id=1, source_target_pairs={{0,0},{8,32},{16,8},{24,40},{32,16},{40,48},{48,24},{56,56},{64,72... | collective-permute-start | bytes 3145736 | tf_op jit(solution)/shard_map/rows_along_z/ppermute | solution.py:248
  188.0 41.8 %collective-permute-start.25 = (f32[256,1024]{1,0:T(8,128)S(1)}, f32[256,1024]{1,0:T(8,128)S(1)}, u32[]{:S(2)}, u32[]{:S(2)}) collective-permute-start(f32[256,1024]{1,0:T(8,128)S(1)} %convolution_subtract_fusion), channel_id=1, source_target_pairs={{0,192},{8,136},{16,80},{24,24},{32,224},{40,168},{48,112},{56,56}... | collective-permute-start | bytes 3145736 | tf_op jit(solution)/shard_map/to_parent/ppermute | solution.py:278
  193.4 36.5 %collective-permute-start.23 = (f32[256,1024]{1,0:T(8,128)S(1)}, f32[256,1024]{1,0:T(8,128)S(1)}, u32[]{:S(2)}, u32[]{:S(2)}) collective-permute-start(f32[256,1024]{1,0:T(8,128)S(1)} %convolution_subtract_fusion.1), channel_id=1, source_target_pairs={{0,128},{8,200},{16,16},{24,88},{32,160},{40,232},{48,48},{56,120}... | collective-permute-start | bytes 3145736 | tf_op jit(solution)/shard_map/to_parent/ppermute | solution.py:278
  196.5 33.4 %collective-permute-start.21 = (f32[256,1024]{1,0:T(8,128)S(1)}, f32[256,1024]{1,0:T(8,128)S(1)}, u32[]{:S(2)}, u32[]{:S(2)}) collective-permute-start(f32[256,1024]{1,0:T(8,128)S(1)} %convolution_subtract_fusion.2), channel_id=1, source_target_pairs={{0,64},{8,8},{16,208},{24,152},{32,96},{40,40},{48,240},{56,184},{... | collective-permute-start | bytes 3145736 | tf_op jit(solution)/shard_map/to_parent/ppermute | solution.py:278
  219.0 40.6 %collective-permute-start.19 = (f32[256,1024]{1,0:T(8,128)S(1)}, f32[256,1024]{1,0:T(8,128)}, u32[]{:S(2)}, u32[]{:S(2)}) collective-permute-start(f32[256,1024]{1,0:T(8,128)S(1)} %convolution_subtract_fusion.3), channel_id=1, source_target_pairs={{0,0},{8,72},{16,144},{24,216},{32,32},{40,104},{48,176},{56,248},... | collective-permute-start | bytes 3145736 | tf_op jit(solution)/shard_map/to_parent/ppermute | solution.py:278
  229.8 29.8 %copy-start.3 = (f32[256,1024]{1,0:T(8,128)}, f32[256,1024]{1,0:T(8,128)S(1)}, u32[]{:S(2)}) copy-start(f32[256,1024]{1,0:T(8,128)S(1)} %collective-permute-done.25.refs_3_) | copy-start | bytes 3145732
  229.9 29.8 %copy-start.4 = (f32[256,1024]{1,0:T(8,128)}, f32[256,1024]{1,0:T(8,128)S(1)}, u32[]{:S(2)}) copy-start(f32[256,1024]{1,0:T(8,128)S(1)} %collective-permute-done.23.refs_2_) | copy-start | bytes 3145732
  (3 other events, 32.6 us)
Sparse Core Ops, SparseCore 0:
  25.0 55.1 all-gather.4
  82.0 36.8 all-gather.6
  120.7 57.4 all-gather.8

commit v4 on v3

--- a/solution.py
+++ b/solution.py
@@ -235,17 +235,17 @@
         panel_top = lax.all_gather(panel_part, "row", tiled=True)
 
     with jax.named_scope("rows_along_z"):
-        panel_top, matrix = lax.optimization_barrier((panel_top, matrix))
+        pieces = [(my_row // 2) ^ k ^ my_front for k in range(PIECES)]
+        sent = [lax.dynamic_slice_in_dim(matrix, piece * PIECE, PIECE, 0) for piece in pieces]
+        panel_top, *sent = lax.optimization_barrier((panel_top, *sent))
         arrived = []
         for k in range(PIECES):
-            piece = (my_row // 2) ^ k ^ my_front
-            sent = lax.dynamic_slice_in_dim(matrix, piece * PIECE, PIECE, 0)
             pairs = [
                 (f * 8 + r, f * 8 + 4 * (r % 2) + ((r // 2) ^ k ^ f))
                 for f in range(4)
                 for r in range(8)
             ]
-            arrived.append(lax.ppermute(sent, FRONT_AXES, pairs))
+            arrived.append(lax.ppermute(sent[k], FRONT_AXES, pairs))
 
     with jax.named_scope("row_panel"):
         half = my_col & 1

time: 275 us -> 277 us (level)
  the two profiles are of different devices: /device:TPU:91 before, /device:TPU:6 now
where the time goes in v4:
time: 277 us; the launch traced here: 275 us
  waiting for transfers between devices  143 us (52%)
  starting transfers between devices  61.1 us (22%)
  Pallas kernels  30.8 us (11%)
  between operations  13.6 us (5%)
  local copies, waits for them, and re-layouts  11.1 us (4%)
  matrix products  9.35 us (3%)
  other arithmetic  5.85 us (2%)
    all_gather x1, waiting for transfers between devices, local(): row_panel = lax.all_gather(mine, 'col')  33.9 us
    ppermute x4, waiting for transfers between devices, local(): pieces.append(lax.ppermute(schur, FRONT_AXES, pairs))  32.4 us
    ppermute x14, waiting for transfers between devices, fan_out(): received = [lax.ppermute(parts[k], axis, [numbers(k)]) for k in range(1, 8)]  30.8 us
    ppermute x4, starting transfers between devices, local(): arrived.append(lax.ppermute(sent[k], FRONT_AXES, pairs))  22.5 us
    ppermute x14, starting transfers between devices, fan_out(): received = [lax.ppermute(parts[k], axis, [numbers(k)]) for k in range(1, 8)]  20.9 us
    pallas_call x1, Pallas kernels, inverse_factor(): pl.pallas_call(factor_kernel, out_shape=jax.ShapeDtypeStruct((PANEL, PANE...  18 us
    ppermute x3, waiting for transfers between devices, local(): far = lax.ppermute(part, 'row', pairs)  17.5 us
    ppermute x4, waiting for transfers between devices, local(): arrived.append(lax.ppermute(sent[k], FRONT_AXES, pairs))  13.8 us
  transfers between devices with their start and end apart: 29, of which 16 were waited for; matrix products, arithmetic and copies ran while one was open for 7% of the time, Pallas kernels for 9%

profile of v4, /device:TPU:6, one launch (start us, length us, event | category | flops | bytes accessed | tf_op | source)
XLA Modules:
  0.0 274.9 jit_solution(4952614027500165005)
XLA Ops:
  8.1 7.8 %collective-permute-start.6 = (f32[64,1024]{1,0:T(8,128)S(1)}, f32[64,1024]{1,0:T(8,128)S(1)}, u32[]{:S(2)}, u32[]{:S(2)}) collective-permute-start(f32[64,1024]{1,0:T(8,128)S(1)} %get-tuple-element.31), channel_id=1, source_target_pairs={{0,56},{1,57},{2,58},{3,59},{4,60},{5,61},{6,62},{7,63},{64,120},{... | collective-permute-start | bytes 786440 | tf_op jit(solution)/shard_map/panel_scatter/ppermute | solution.py:201
  23.9 4.3 %collective-permute-done.5 = f32[64,1024]{1,0:T(8,128)S(1)} collective-permute-done((f32[64,1024]{1,0:T(8,128)S(1)}, f32[64,1024]{1,0:T(8,128)S(1)}, u32[]{:S(2)}, u32[]{:S(2)}) %collective-permute-start.5) | collective-permute-done | bytes 262176 | tf_op jit(solution)/shard_map/panel_scatter/ppermute | solution.py:201
  29.5 3.2 %collective-permute-done.4 = f32[64,1024]{1,0:T(8,128)S(1)} collective-permute-done((f32[64,1024]{1,0:T(8,128)S(1)}, f32[64,1024]{1,0:T(8,128)S(1)}, u32[]{:S(2)}, u32[]{:S(2)}) %collective-permute-start.4) | collective-permute-done | bytes 262176 | tf_op jit(solution)/shard_map/panel_scatter/ppermute | solution.py:201
  32.7 5.1 %collective-permute-done = f32[64,1024]{1,0:T(8,128)S(1)} collective-permute-done((f32[64,1024]{1,0:T(8,128)S(1)}, f32[64,1024]{1,0:T(8,128)S(1)}, u32[]{:S(2)}, u32[]{:S(2)}) %collective-permute-start) | collective-permute-done | bytes 262176 | tf_op jit(solution)/shard_map/panel_scatter/ppermute | solution.py:201
  37.7 4.5 %collective-permute-done.1 = f32[64,1024]{1,0:T(8,128)S(1)} collective-permute-done((f32[64,1024]{1,0:T(8,128)S(1)}, f32[64,1024]{1,0:T(8,128)S(1)}, u32[]{:S(2)}, u32[]{:S(2)}) %collective-permute-start.1) | collective-permute-done | bytes 262176 | tf_op jit(solution)/shard_map/panel_scatter/ppermute | solution.py:201
  42.2 1.8 bitcast_select_fusion
  50.8 12.3 %collective-permute-done.8 = f32[64,512]{1,0:T(8,128)S(1)} collective-permute-done((f32[64,512]{1,0:T(8,128)S(1)}, f32[64,512]{1,0:T(8,128)S(1)}, u32[]{:S(2)}, u32[]{:S(2)}) %collective-permute-start.8) | collective-permute-done | bytes 131104 | tf_op jit(solution)/shard_map/pivot_to_columns/ppermute | solution.py:201
  65.5 6.1 %collective-permute-done.15 = f32[64,512]{1,0:T(8,128)S(1)} collective-permute-done((f32[64,512]{1,0:T(8,128)S(1)}, f32[64,512]{1,0:T(8,128)S(1)}, u32[]{:S(2)}, u32[]{:S(2)}) %collective-permute-start.15) | collective-permute-done | bytes 131104 | tf_op jit(solution)/shard_map/pivot_along_z/ppermute | solution.py:228
  72.9 6.0 %collective-permute-done.16 = f32[64,512]{1,0:T(8,128)S(1)} collective-permute-done((f32[64,512]{1,0:T(8,128)S(1)}, f32[64,512]{1,0:T(8,128)S(1)}, u32[]{:S(2)}, u32[]{:S(2)}) %collective-permute-start.16) | collective-permute-done | bytes 131104 | tf_op jit(solution)/shard_map/pivot_along_z/ppermute | solution.py:228
  80.2 5.4 %collective-permute-done.17 = f32[64,512]{1,0:T(8,128)S(1)} collective-permute-done((f32[64,512]{1,0:T(8,128)S(1)}, f32[64,512]{1,0:T(8,128)S(1)}, u32[]{:S(2)}, u32[]{:S(2)}) %collective-permute-start.17) | collective-permute-done | bytes 131104 | tf_op jit(solution)/shard_map/pivot_along_z/ppermute | solution.py:228
  86.4 4.4 %dynamic-slice_bitcast_fusion = (f32[256,1024]{1,0:T(8,128)}, f32[256,1024]{1,0:T(8,128)}, f32[256,1024]{1,0:T(8,128)}, f32[256,1024]{1,0:T(8,128)}) fusion(f32[1,1024,1024]{2,1,0:T(8,128)} %param.3, s32[]{:T(128)S(6)} %select_n.89, s32[]{:T(128)S(6)} %select_n.88, s32[]{:T(128)S(6)} %select_n.87, s32[]{:T(128)S(6)} %select_n.86), kind=kLoop, calls=%fused_computation.4 | loop fusion | bytes 8388624 | tf_op jit(solution)/shard_map/rows_along_z/dynamic_slice | solution.py:239
  93.1 6.9 %collective-permute-done.18 = f32[512,128]{1,0:T(8,128)S(1)} collective-permute-done((f32[512,128]{1,0:T(8,128)S(1)}, f32[512,128]{1,0:T(8,128)S(1)}, u32[]{:S(2)}, u32[]{:S(2)}) %collective-permute-start.18) | collective-permute-done | bytes 262176 | tf_op jit(solution)/shard_map/row_panel/ppermute | solution.py:258
  100.0 1.7 dynamic-slice_select_fusion
  101.7 3.8 %collective-permute-start.7 = (f32[256,1024]{1,0:T(8,128)}, f32[256,1024]{1,0:T(8,128)}, u32[]{:S(2)}, u32[]{:S(2)}) collective-permute-start(f32[256,1024]{1,0:T(8,128)} %get-tuple-element.12), channel_id=1, source_target_pairs={{0,0},{8,32},{16,8},{24,40},{32,16},{40,48},{48,24},{56,56},{64,72... | collective-permute-start | bytes 3145736 | tf_op jit(solution)/shard_map/rows_along_z/ppermute | solution.py:248
  105.5 5.8 %collective-permute-start.20 = (f32[256,1024]{1,0:T(8,128)}, f32[256,1024]{1,0:T(8,128)}, u32[]{:S(2)}, u32[]{:S(2)}) collective-permute-start(f32[256,1024]{1,0:T(8,128)} %get-tuple-element.16), channel_id=1, source_target_pairs={{0,8},{8,40},{16,0},{24,32},{32,24},{40,56},{48,16},{56,48},{64,64... | collective-permute-start | bytes 3145736 | tf_op jit(solution)/shard_map/rows_along_z/ppermute | solution.py:248
  111.3 9.5 %collective-permute-start.22 = (f32[256,1024]{1,0:T(8,128)}, f32[256,1024]{1,0:T(8,128)}, u32[]{:S(2)}, u32[]{:S(2)}) collective-permute-start(f32[256,1024]{1,0:T(8,128)} %get-tuple-element.17), channel_id=1, source_target_pairs={{0,16},{8,48},{16,24},{24,56},{32,0},{40,32},{48,8},{56,40},{64,88... | collective-permute-start | bytes 3145736 | tf_op jit(solution)/shard_map/rows_along_z/ppermute | solution.py:248
  120.8 7.8 %all-gather.7.cloned.1.call-done.pivot_ref = f32[512,512]{1,0:T(8,128)} async-done(((f32[64,512]{1,0:T(8,128)}), f32[512,512]{1,0:T(8,128)}) %all-gather.7.cloned.1.call-update) | async-done | bytes 1048592 | tf_op jit(solution)/shard_map/pivot_in_plane/all_gather | solution.py:232
  129.8 18.0 %inverse_factor.1.inverse_ref = f32[512,512]{1,0:T(8,128)S(1)} custom-call(f32[512,512]{1,0:T(8,128)S(1)} %copy-done), custom_call_target="tpu_custom_call" | custom-call | flops 300000000 | bytes 2097152 | tf_op jit(solution)/shard_map/factor/inverse_factor/pallas_call | solution.py:92
  147.9 3.4 %collective-permute-start.24 = (f32[256,1024]{1,0:T(8,128)}, f32[256,1024]{1,0:T(8,128)}, u32[]{:S(2)}, u32[]{:S(2)}) collective-permute-start(f32[256,1024]{1,0:T(8,128)} %get-tuple-element.18), channel_id=1, source_target_pairs={{0,24},{8,56},{16,16},{24,48},{32,8},{40,40},{48,0},{56,32},{64,80... | collective-permute-start | bytes 3145736 | tf_op jit(solution)/shard_map/rows_along_z/ppermute | solution.py:248
  151.3 33.9 %all-gather.9.cloned.1.call-done = f32[4096,128]{1,0:T(8,128)} async-done(((f32[512,128]{1,0:T(8,128)}), f32[4096,128]{1,0:T(8,128)}) %all-gather.9.cloned.1.call-update) | async-done | bytes 2097168 | tf_op jit(solution)/shard_map/row_panel/all_gather | solution.py:260
  186.8 5.8 %solve.1 = (f32[1024,512]{1,0:T(8,128)S(1)}, f32[512,1024]{1,0:T(8,128)S(1)}) custom-call(f32[512,512]{1,0:T(8,128)S(1)} %inverse_factor.1.inverse_ref, f32[512,1024]{1,0:T(8,128)S(1)} %copy-done.1, f32[8,512,128]{2,1,0:T(8,128)S(1)} %bitcast.33), custom_call_target="tpu_custom_call" | custom-call | flops 3000000000 | bytes 9437184 | tf_op jit(solution)/shard_map/solve/solve/pallas_call | solution.py:133
  192.7 2.3 convolution_subtract_fusion.3
  195.7 7.0 %collective-permute-done.20 = f32[256,1024]{1,0:T(8,128)} collective-permute-done((f32[256,1024]{1,0:T(8,128)}, f32[256,1024]{1,0:T(8,128)}, u32[]{:S(2)}, u32[]{:S(2)}) %collective-permute-start.20) | collective-permute-done | bytes 1048608 | tf_op jit(solution)/shard_map/rows_along_z/ppermute | solution.py:248
  202.8 2.3 convolution_subtract_fusion.2
  205.1 1.9 collective-permute-start.21
  207.1 2.3 convolution_subtract_fusion.1
  209.4 1.9 collective-permute-start.23
  211.3 6.8 %collective-permute-done.24 = f32[256,1024]{1,0:T(8,128)} collective-permute-done((f32[256,1024]{1,0:T(8,128)}, f32[256,1024]{1,0:T(8,128)}, u32[]{:S(2)}, u32[]{:S(2)}) %collective-permute-start.24) | collective-permute-done | bytes 1048608 | tf_op jit(solution)/shard_map/rows_along_z/ppermute | solution.py:248
  218.1 2.3 convolution_subtract_fusion
  220.5 7.9 %collective-permute-start.25 = (f32[256,1024]{1,0:T(8,128)S(1)}, f32[256,1024]{1,0:T(8,128)}, u32[]{:S(2)}, u32[]{:S(2)}) collective-permute-start(f32[256,1024]{1,0:T(8,128)S(1)} %convolution_subtract_fusion), channel_id=1, source_target_pairs={{0,192},{8,136},{16,80},{24,24},{32,224},{40,168},{48,112},{56,56}... | collective-permute-start | bytes 3145736 | tf_op jit(solution)/shard_map/to_parent/ppermute | solution.py:278
  229.9 31.6 %collective-permute-done.25.refs_3_ = f32[256,1024]{1,0:T(8,128)} collective-permute-done((f32[256,1024]{1,0:T(8,128)S(1)}, f32[256,1024]{1,0:T(8,128)}, u32[]{:S(2)}, u32[]{:S(2)}) %collective-permute-start.25) | collective-permute-done | bytes 1048608 | tf_op jit(solution)/shard_map/to_parent/ppermute | solution.py:278
  261.4 6.9 %extend_add.1 = f32[512,2048]{1,0:T(8,128)} custom-call(s32[3]{0:T(128)} %pad_add_fusion.place_ref, s32[4,60]{1,0:T(4,128)} %map_ref.1, f32[512,2048]{1,0:T(8,128)} %parent_ref.1, f32[256,1024]{1,0:T(8,128)} %copy-done.3, f32[256,1024]{1,0:T(8,128)} %copy-done.4, f32[256,1024]{1,0:T(8,128)} %copy-done.5, f32[256,1024]{1,0:T(8,128)} %collective-permute-done.25.refs_3_), custom_call_target="tpu_custom_call" | custom-call | flops 8388608 | bytes 12582912 | tf_op jit(solution)/shard_map/extend_add/extend_add/pallas_call | solution.py:184
  (59 shorter events, 30.5 us)
Async XLA Ops:
  6.5 84.2 %all-gather.5.cloned.1.call-start = ((), (), s32[]{:S(2)}) async-start(), calls=%async_computation | async-start | bytes 2359296 | tf_op jit(solution)/shard_map/panel_gather/all_gather | solution.py:235
  8.1 14.5 %collective-permute-start.6 = (f32[64,1024]{1,0:T(8,128)S(1)}, f32[64,1024]{1,0:T(8,128)S(1)}, u32[]{:S(2)}, u32[]{:S(2)}) collective-permute-start(f32[64,1024]{1,0:T(8,128)S(1)} %get-tuple-element.31), channel_id=1, source_target_pairs={{0,56},{1,57},{2,58},{3,59},{4,60},{5,61},{6,62},{7,63},{64,120},{... | collective-permute-start | bytes 786440 | tf_op jit(solution)/shard_map/panel_scatter/ppermute | solution.py:201
  15.9 12.3 %collective-permute-start.5 = (f32[64,1024]{1,0:T(8,128)S(1)}, f32[64,1024]{1,0:T(8,128)S(1)}, u32[]{:S(2)}, u32[]{:S(2)}) collective-permute-start(f32[64,1024]{1,0:T(8,128)S(1)} %get-tuple-element.32), channel_id=1, source_target_pairs={{0,48},{1,49},{2,50},{3,51},{4,52},{5,53},{6,54},{7,55},{64,112},{... | collective-permute-start | bytes 786440 | tf_op jit(solution)/shard_map/panel_scatter/ppermute | solution.py:201
  17.2 15.5 %collective-permute-start.4 = (f32[64,1024]{1,0:T(8,128)S(1)}, f32[64,1024]{1,0:T(8,128)S(1)}, u32[]{:S(2)}, u32[]{:S(2)}) collective-permute-start(f32[64,1024]{1,0:T(8,128)S(1)} %get-tuple-element.33), channel_id=1, source_target_pairs={{0,40},{1,41},{2,42},{3,43},{4,44},{5,45},{6,46},{7,47},{64,104},{... | collective-permute-start | bytes 786440 | tf_op jit(solution)/shard_map/panel_scatter/ppermute | solution.py:201
  18.5 14.1 %collective-permute-start.3 = (f32[64,1024]{1,0:T(8,128)S(1)}, f32[64,1024]{1,0:T(8,128)S(1)}, u32[]{:S(2)}, u32[]{:S(2)}) collective-permute-start(f32[64,1024]{1,0:T(8,128)S(1)} %get-tuple-element.34), channel_id=1, source_target_pairs={{0,32},{1,33},{2,34},{3,35},{4,36},{5,37},{6,38},{7,39},{64,96},{6... | collective-permute-start | bytes 786440 | tf_op jit(solution)/shard_map/panel_scatter/ppermute | solution.py:201
  19.8 12.8 %collective-permute-start.2 = (f32[64,1024]{1,0:T(8,128)S(1)}, f32[64,1024]{1,0:T(8,128)S(1)}, u32[]{:S(2)}, u32[]{:S(2)}) collective-permute-start(f32[64,1024]{1,0:T(8,128)S(1)} %get-tuple-element.35), channel_id=1, source_target_pairs={{0,24},{1,25},{2,26},{3,27},{4,28},{5,29},{6,30},{7,31},{64,88},{6... | collective-permute-start | bytes 786440 | tf_op jit(solution)/shard_map/panel_scatter/ppermute | solution.py:201
  22.6 15.2 %collective-permute-start = (f32[64,1024]{1,0:T(8,128)S(1)}, f32[64,1024]{1,0:T(8,128)S(1)}, u32[]{:S(2)}, u32[]{:S(2)}) collective-permute-start(f32[64,1024]{1,0:T(8,128)S(1)} %get-tuple-element.36), channel_id=1, source_target_pairs={{0,8},{1,9},{2,10},{3,11},{4,12},{5,13},{6,14},{7,15},{64,72},{65,... | collective-permute-start | bytes 786440 | tf_op jit(solution)/shard_map/panel_scatter/ppermute | solution.py:201
  28.2 14.0 %collective-permute-start.1 = (f32[64,1024]{1,0:T(8,128)S(1)}, f32[64,1024]{1,0:T(8,128)S(1)}, u32[]{:S(2)}, u32[]{:S(2)}) collective-permute-start(f32[64,1024]{1,0:T(8,128)S(1)} %get-tuple-element.30), channel_id=1, source_target_pairs={{0,16},{1,17},{2,18},{3,19},{4,20},{5,21},{6,22},{7,23},{64,80},{6... | collective-permute-start | bytes 786440 | tf_op jit(solution)/shard_map/panel_scatter/ppermute | solution.py:201
  44.0 84.6 %all-gather.7.cloned.1.call-start = ((), (), s32[]{:S(2)}) async-start(), calls=%async_computation.1 | async-start | bytes 1179648 | tf_op jit(solution)/shard_map/pivot_in_plane/all_gather | solution.py:232
  45.4 3.4 %collective-permute-start.14 = (f32[64,512]{1,0:T(8,128)S(1)}, f32[64,512]{1,0:T(8,128)S(1)}, u32[]{:S(2)}, u32[]{:S(2)}) collective-permute-start(f32[64,512]{1,0:T(8,128)S(1)} %get-tuple-element.20), channel_id=1, source_target_pairs={{0,7},{64,71},{128,135},{192,199}} | collective-permute-start | bytes 393224 | tf_op jit(solution)/shard_map/pivot_to_columns/ppermute | solution.py:201
  46.1 4.0 %collective-permute-start.13 = (f32[64,512]{1,0:T(8,128)S(1)}, f32[64,512]{1,0:T(8,128)S(1)}, u32[]{:S(2)}, u32[]{:S(2)}) collective-permute-start(f32[64,512]{1,0:T(8,128)S(1)} %get-tuple-element.21), channel_id=1, source_target_pairs={{0,6},{64,70},{128,134},{192,198}} | collective-permute-start | bytes 393224 | tf_op jit(solution)/shard_map/pivot_to_columns/ppermute | solution.py:201
  46.8 4.0 %collective-permute-start.12 = (f32[64,512]{1,0:T(8,128)S(1)}, f32[64,512]{1,0:T(8,128)S(1)}, u32[]{:S(2)}, u32[]{:S(2)}) collective-permute-start(f32[64,512]{1,0:T(8,128)S(1)} %get-tuple-element.22), channel_id=1, source_target_pairs={{0,5},{64,69},{128,133},{192,197}} | collective-permute-start | bytes 393224 | tf_op jit(solution)/shard_map/pivot_to_columns/ppermute | solution.py:201
  47.5 3.4 %collective-permute-start.11 = (f32[64,512]{1,0:T(8,128)S(1)}, f32[64,512]{1,0:T(8,128)S(1)}, u32[]{:S(2)}, u32[]{:S(2)}) collective-permute-start(f32[64,512]{1,0:T(8,128)S(1)} %get-tuple-element.23), channel_id=1, source_target_pairs={{0,4},{64,68},{128,132},{192,196}} | collective-permute-start | bytes 393224 | tf_op jit(solution)/shard_map/pivot_to_columns/ppermute | solution.py:201
  48.1 2.7 collective-permute-start.10
  48.8 14.3 %collective-permute-start.8 = (f32[64,512]{1,0:T(8,128)S(1)}, f32[64,512]{1,0:T(8,128)S(1)}, u32[]{:S(2)}, u32[]{:S(2)}) collective-permute-start(f32[64,512]{1,0:T(8,128)S(1)} %get-tuple-element.25), channel_id=1, source_target_pairs={{0,1},{64,65},{128,129},{192,193}} | collective-permute-start | bytes 393224 | tf_op jit(solution)/shard_map/pivot_to_columns/ppermute | solution.py:201
  50.1 13.0 %collective-permute-start.9 = (f32[64,512]{1,0:T(8,128)S(1)}, f32[64,512]{1,0:T(8,128)S(1)}, u32[]{:S(2)}, u32[]{:S(2)}) collective-permute-start(f32[64,512]{1,0:T(8,128)S(1)} %get-tuple-element.19), channel_id=1, source_target_pairs={{0,2},{64,66},{128,130},{192,194}} | collective-permute-start | bytes 393224 | tf_op jit(solution)/shard_map/pivot_to_columns/ppermute | solution.py:201
  64.2 7.4 %collective-permute-start.15 = (f32[64,512]{1,0:T(8,128)S(1)}, f32[64,512]{1,0:T(8,128)S(1)}, u32[]{:S(2)}, u32[]{:S(2)}) collective-permute-start(f32[64,512]{1,0:T(8,128)S(1)} %slice_select_fusion), channel_id=1, source_target_pairs={{0,32},{1,33},{2,34},{3,35},{4,36},{5,37},{6,38},{7,39},{64,96},{6... | collective-permute-start | bytes 393224 | tf_op jit(solution)/shard_map/pivot_along_z/ppermute | solution.py:228
  71.6 7.3 %collective-permute-start.16 = (f32[64,512]{1,0:T(8,128)S(1)}, f32[64,512]{1,0:T(8,128)S(1)}, u32[]{:S(2)}, u32[]{:S(2)}) collective-permute-start(f32[64,512]{1,0:T(8,128)S(1)} %broadcast_select_fusion), channel_id=1, source_target_pairs={{0,16},{32,48},{1,17},{33,49},{2,18},{34,50},{3,19},{35,51},{4,20}... | collective-permute-start | bytes 393224 | tf_op jit(solution)/shard_map/pivot_along_z/ppermute | solution.py:228
  78.9 6.7 %collective-permute-start.17 = (f32[64,512]{1,0:T(8,128)S(1)}, f32[64,512]{1,0:T(8,128)S(1)}, u32[]{:S(2)}, u32[]{:S(2)}) collective-permute-start(f32[64,512]{1,0:T(8,128)S(1)} %broadcast_select_fusion.1), channel_id=1, source_target_pairs={{0,8},{16,24},{32,40},{48,56},{1,9},{17,25},{33,41},{49,57},{2,10}... | collective-permute-start | bytes 393224 | tf_op jit(solution)/shard_map/pivot_along_z/ppermute | solution.py:228
  86.3 98.9 %all-gather.9.cloned.1.call-start = ((), (), s32[]{:S(2)}) async-start(), calls=%async_computation.2 | async-start | bytes 2359296 | tf_op jit(solution)/shard_map/row_panel/all_gather | solution.py:260
  91.7 8.3 %collective-permute-start.18 = (f32[512,128]{1,0:T(8,128)S(1)}, f32[512,128]{1,0:T(8,128)S(1)}, u32[]{:S(2)}, u32[]{:S(2)}) collective-permute-start(f32[512,128]{1,0:T(8,128)S(1)} %constant_dynamic-slice_fusion), channel_id=1, source_target_pairs={{0,1},{2,3},{4,5},{6,7},{8,9},{10,11},{12,13},{14,15},{16,17},{18,... | collective-permute-start | bytes 786440 | tf_op jit(solution)/shard_map/row_panel/ppermute | solution.py:258
  101.7 90.9 %collective-permute-start.7 = (f32[256,1024]{1,0:T(8,128)}, f32[256,1024]{1,0:T(8,128)}, u32[]{:S(2)}, u32[]{:S(2)}) collective-permute-start(f32[256,1024]{1,0:T(8,128)} %get-tuple-element.12), channel_id=1, source_target_pairs={{0,0},{8,32},{16,8},{24,40},{32,16},{40,48},{48,24},{56,56},{64,72... | collective-permute-start | bytes 3145736 | tf_op jit(solution)/shard_map/rows_along_z/ppermute | solution.py:248
  105.5 97.3 %collective-permute-start.20 = (f32[256,1024]{1,0:T(8,128)}, f32[256,1024]{1,0:T(8,128)}, u32[]{:S(2)}, u32[]{:S(2)}) collective-permute-start(f32[256,1024]{1,0:T(8,128)} %get-tuple-element.16), channel_id=1, source_target_pairs={{0,8},{8,40},{16,0},{24,32},{32,24},{40,56},{48,16},{56,48},{64,64... | collective-permute-start | bytes 3145736 | tf_op jit(solution)/shard_map/rows_along_z/ppermute | solution.py:248
  111.3 95.8 %collective-permute-start.22 = (f32[256,1024]{1,0:T(8,128)}, f32[256,1024]{1,0:T(8,128)}, u32[]{:S(2)}, u32[]{:S(2)}) collective-permute-start(f32[256,1024]{1,0:T(8,128)} %get-tuple-element.17), channel_id=1, source_target_pairs={{0,16},{8,48},{16,24},{24,56},{32,0},{40,32},{48,8},{56,40},{64,88... | collective-permute-start | bytes 3145736 | tf_op jit(solution)/shard_map/rows_along_z/ppermute | solution.py:248
  129.8 55.4 %copy-start.1 = (f32[512,1024]{1,0:T(8,128)S(1)}, f32[512,1024]{1,0:T(8,128)}, u32[]{:S(2)}) copy-start(f32[512,1024]{1,0:T(8,128)} %all-gather.5.cloned.1.call-done.top_ref) | copy-start | bytes 6291460
  147.9 70.2 %collective-permute-start.24 = (f32[256,1024]{1,0:T(8,128)}, f32[256,1024]{1,0:T(8,128)}, u32[]{:S(2)}, u32[]{:S(2)}) collective-permute-start(f32[256,1024]{1,0:T(8,128)} %get-tuple-element.18), channel_id=1, source_target_pairs={{0,24},{8,56},{16,16},{24,48},{32,8},{40,40},{48,0},{56,32},{64,80... | collective-permute-start | bytes 3145736 | tf_op jit(solution)/shard_map/rows_along_z/ppermute | solution.py:248
  195.0 34.0 %collective-permute-start.19 = (f32[256,1024]{1,0:T(8,128)S(1)}, f32[256,1024]{1,0:T(8,128)S(1)}, u32[]{:S(2)}, u32[]{:S(2)}) collective-permute-start(f32[256,1024]{1,0:T(8,128)S(1)} %convolution_subtract_fusion.3), channel_id=1, source_target_pairs={{0,0},{8,72},{16,144},{24,216},{32,32},{40,104},{48,176},{56,248},... | collective-permute-start | bytes 3145736 | tf_op jit(solution)/shard_map/to_parent/ppermute | solution.py:278
  205.1 23.9 %collective-permute-start.21 = (f32[256,1024]{1,0:T(8,128)S(1)}, f32[256,1024]{1,0:T(8,128)S(1)}, u32[]{:S(2)}, u32[]{:S(2)}) collective-permute-start(f32[256,1024]{1,0:T(8,128)S(1)} %convolution_subtract_fusion.2), channel_id=1, source_target_pairs={{0,64},{8,8},{16,208},{24,152},{32,96},{40,40},{48,240},{56,184},{... | collective-permute-start | bytes 3145736 | tf_op jit(solution)/shard_map/to_parent/ppermute | solution.py:278
  209.4 20.4 %collective-permute-start.23 = (f32[256,1024]{1,0:T(8,128)S(1)}, f32[256,1024]{1,0:T(8,128)S(1)}, u32[]{:S(2)}, u32[]{:S(2)}) collective-permute-start(f32[256,1024]{1,0:T(8,128)S(1)} %convolution_subtract_fusion.1), channel_id=1, source_target_pairs={{0,128},{8,200},{16,16},{24,88},{32,160},{40,232},{48,48},{56,120}... | collective-permute-start | bytes 3145736 | tf_op jit(solution)/shard_map/to_parent/ppermute | solution.py:278
  220.5 41.0 %collective-permute-start.25 = (f32[256,1024]{1,0:T(8,128)S(1)}, f32[256,1024]{1,0:T(8,128)}, u32[]{:S(2)}, u32[]{:S(2)}) collective-permute-start(f32[256,1024]{1,0:T(8,128)S(1)} %convolution_subtract_fusion), channel_id=1, source_target_pairs={{0,192},{8,136},{16,80},{24,24},{32,224},{40,168},{48,112},{56,56}... | collective-permute-start | bytes 3145736 | tf_op jit(solution)/shard_map/to_parent/ppermute | solution.py:278
  229.0 32.4 %copy-start.3 = (f32[256,1024]{1,0:T(8,128)}, f32[256,1024]{1,0:T(8,128)S(1)}, u32[]{:S(2)}) copy-start(f32[256,1024]{1,0:T(8,128)S(1)} %collective-permute-done.19.refs_0_) | copy-start | bytes 3145732
  229.0 32.4 %copy-start.4 = (f32[256,1024]{1,0:T(8,128)}, f32[256,1024]{1,0:T(8,128)S(1)}, u32[]{:S(2)}) copy-start(f32[256,1024]{1,0:T(8,128)S(1)} %collective-permute-done.21.refs_1_) | copy-start | bytes 3145732
  (3 other events, 34.4 us)
Sparse Core Ops, SparseCore 0:
  44.2 43.7 all-gather.4
  89.8 38.8 all-gather.6
  130.4 54.7 all-gather.8
